TPU v7x, 32 devices: a whole 2x2x4 slice. The times are simulated.
32 devices in a mesh: ta: 4 (over y, x), ha: 2 (over core), wa: 4 (over z).
Axes of the slice: x: 2, y: 2, z: 4, core: 2. Of those that a mesh axis runs over, the one named last changes fastest.
Arguments:
- latents: bfloat16 [8, 32, 128, 256], P('ta', 'ha', 'wa'), may hold values from -6 to 6
- norm_gain: float32 [256], replicated, may hold values from 0.1 to 1.9
- conv_weight: bfloat16 [3, 3, 3, 256, 256], replicated, may hold values from -0.078125 to 0.078125
- qkv_weight: bfloat16 [1024, 16, 3, 128], P(None, ('ta', 'wa')), may hold values from -2.7 to 2.7
Outputs:
- block_out: bfloat16 [8, 32, 128, 256], P('ta', 'ha', 'wa')
- attended: bfloat16 [8, 16, 64, 16, 128], P(None, 'ha', None, ('ta', 'wa'))
All inputs are finite; a program needn't handle non-finite values.
Results may differ from a plain program's by a relative error of at most 0.0062.
Values may be sent and summed in bfloat16 or wider, within the bound.
A program may use at most 128 MiB of HBM per device.

v0:
```python
import jax
import jax.numpy as jnp
from jax import lax
from jax.sharding import PartitionSpec as P

WIN = 4


def extended(cells, sides, width):
    for axis, dim in sides:
        count = lax.axis_size(axis)
        ends = count - 1
        head = lax.slice_in_dim(cells, 0, width, axis=dim)
        tail = lax.slice_in_dim(cells, cells.shape[dim] - width, cells.shape[dim], axis=dim)
        cells = jnp.concatenate(
            [
                lax.ppermute(tail, axis, [(i, (i + 1) % count) for i in range(ends)]),
                cells,
                lax.ppermute(head, axis, [((i + 1) % count, i) for i in range(ends)]),
            ],
            axis=dim,
        )
    return cells


def local(latents, norm_gain, conv_weight, qkv_weight):
    t_dev, h_dev, w_dev, channels = latents.shape
    rows_dev = h_dev // 2
    cols_dev = w_dev // 2
    latent_f32 = latents.astype(jnp.float32)
    scale_rms = lax.rsqrt(jnp.mean(latent_f32 * latent_f32, axis=-1, keepdims=True) + 1e-06)
    normed = jax.nn.silu(latent_f32 * scale_rms * norm_gain).astype(jnp.bfloat16)
    padded = extended(normed, (("ta", 0), ("ha", 1), ("wa", 2)), 1)
    conv_out = lax.conv_general_dilated(
        padded[None],
        conv_weight,
        (1, 1, 1),
        "VALID",
        dimension_numbers=("NDHWC", "DHWIO", "NDHWC"),
        preferred_element_type=jnp.float32,
    )[0]
    block_out = (latent_f32 + conv_out).astype(jnp.bfloat16)
    patches = (
        block_out.reshape(t_dev, rows_dev, 2, cols_dev, 2, channels)
        .transpose(0, 1, 3, 2, 4, 5)
        .reshape(t_dev * rows_dev * cols_dev, 4 * channels)
    )
    width_in, head_dev, qkv_count, head_size = qkv_weight.shape
    own_weight = qkv_weight.reshape(width_in, -1)
    gathered = jnp.dot(
        lax.all_gather(patches, ("ta", "wa"), axis=0, tiled=True),
        own_weight,
        preferred_element_type=jnp.float32,
    ).astype(jnp.bfloat16)
    n_time = lax.axis_size("ta")
    n_width = lax.axis_size("wa")
    frames = n_time * t_dev
    patch_cols = n_width * cols_dev
    qkv_rows = gathered.reshape(
        n_time, n_width, t_dev, rows_dev, cols_dev, head_dev, qkv_count, head_size
    )
    qkv_rows = qkv_rows.transpose(0, 2, 3, 1, 4, 5, 6, 7).reshape(
        frames, rows_dev, patch_cols, head_dev, qkv_count, head_size
    )
    queries = qkv_rows[:, :, :, :, 0, :]
    key_value = qkv_rows[:, :, :, :, 1:, :].reshape(
        frames, rows_dev, patch_cols, head_dev, 2 * head_size
    )
    kv_rim = extended(key_value, (("ha", 1),), WIN)
    row_base = lax.axis_index("ha") * rows_dev
    total_rows = rows_dev * lax.axis_size("ha")

    def attend(block_idx):
        q_block = lax.dynamic_slice_in_dim(queries, block_idx * WIN, WIN, 1)
        kv_block = lax.dynamic_slice_in_dim(kv_rim, block_idx * WIN, 3 * WIN, 1)
        key_part = kv_block[..., :head_size]
        value_part = kv_block[..., head_size:]
        scores = jnp.einsum(
            "tiahd,tjbhd->thiajb", q_block, key_part, preferred_element_type=jnp.float32
        ) * head_size ** (-0.5)
        q_row = jnp.arange(WIN, dtype=jnp.int32)[:, None]
        k_row = jnp.arange(3 * WIN, dtype=jnp.int32)[None, :] - WIN
        k_global = row_base + block_idx * WIN + k_row
        allowed = (jnp.abs(q_row - k_row) <= WIN) & (k_global >= 0) & (k_global < total_rows)
        scores = jnp.where(allowed[None, None, :, None, :, None], scores, -1e30)
        row_max = jnp.max(scores, axis=(4, 5), keepdims=True)
        exp_scores = jnp.exp(scores - row_max)
        probs = (exp_scores / jnp.sum(exp_scores, axis=(4, 5), keepdims=True)).astype(jnp.bfloat16)
        result = jnp.einsum(
            "thiajb,tjbhd->tiahd", probs, value_part, preferred_element_type=jnp.float32
        )
        return result.astype(jnp.bfloat16)

    blocks = lax.map(attend, jnp.arange(rows_dev // WIN, dtype=jnp.int32))
    attended = blocks.transpose(1, 0, 2, 3, 4, 5).reshape(
        frames, rows_dev, patch_cols, head_dev, head_size
    )
    return (block_out, attended)


def solution(mesh):
    return jax.shard_map(
        local,
        mesh=mesh,
        in_specs=(P("ta", "ha", "wa", None), P(), P(), P(None, ("ta", "wa"), None, None)),
        out_specs=(P("ta", "ha", "wa", None), P(None, "ha", None, ("ta", "wa"), None)),
        check_vma=False,
    )
```

profile of v0, /device:TPU:0, one launch (start us, length us, event | category | flops | bytes accessed | tf_op | source)
XLA Modules:
  0.0 265.0 jit_solution(1454185686816563368)
XLA Ops:
  10.4 4.9 %collective-permute-start = (bf16[1,16,32,256]{3,1,2,0:T(8,128)(2,1)S(1)}, bf16[1,16,32,256]{3,1,2,0:T(8,128)(2,1)S(1)}, u32[]{:S(2)}, u32[]{:S(2)}) collective-permute-start(bf16[1,16,32,256]{3,1,2,0:T(8,128)(2,1)S(1)} %get-tuple-element.106), channel_id=1, source_target_pairs={{0,8},{8,16},{16,24},{1,9},{9,17},{17,25},{2,10},{10,18},{18,26},{... | collective-permute-start | bytes 786440 | tf_op jit(solution)/shard_map/ppermute | solution.py:17
  16.6 4.2 %collective-permute-done = bf16[1,16,32,256]{3,1,2,0:T(8,128)(2,1)S(1)} collective-permute-done((bf16[1,16,32,256]{3,1,2,0:T(8,128)(2,1)S(1)}, bf16[1,16,32,256]{3,1,2,0:T(8,128)(2,1)S(1)}, u32[]{:S(2)}, u32[]{:S(2)}) %collective-permute-start) | collective-permute-done | bytes 262176 | tf_op jit(solution)/shard_map/ppermute | solution.py:17
  20.8 7.6 %collective-permute-done.1 = bf16[1,16,32,256]{3,1,2,0:T(8,128)(2,1)S(1)} collective-permute-done((bf16[1,16,32,256]{3,1,2,0:T(8,128)(2,1)S(1)}, bf16[1,16,32,256]{3,1,2,0:T(8,128)(2,1)S(1)}, u32[]{:S(2)}, u32[]{:S(2)}) %collective-permute-start.1) | collective-permute-done | bytes 262176 | tf_op jit(solution)/shard_map/ppermute | solution.py:19
  33.2 3.5 %collective-permute-start.4 = (bf16[4,18,1,256]{3,1,2,0:T(8,128)(2,1)S(1)}, bf16[4,18,1,256]{3,1,2,0:T(8,128)(2,1)S(1)}, u32[]{:S(2)}, u32[]{:S(2)}) collective-permute-start(bf16[4,18,1,256]{3,1,2,0:T(8,128)(2,1)S(1)} %get-tuple-element.102), channel_id=1, source_target_pairs={{0,1},{1,2},{2,3},{4,5},{5,6},{6,7},{8,9},{9,10},{10,11},{12,13},{... | collective-permute-start | bytes 110600 | tf_op jit(solution)/shard_map/ppermute | solution.py:17
  38.4 4.3 %collective-permute-done.5 = bf16[4,18,1,256]{3,1,2,0:T(8,128)(2,1)S(1)} collective-permute-done((bf16[4,18,1,256]{3,1,2,0:T(8,128)(2,1)S(1)}, bf16[4,18,1,256]{3,1,2,0:T(8,128)(2,1)S(1)}, u32[]{:S(2)}, u32[]{:S(2)}) %collective-permute-start.5) | collective-permute-done | bytes 36896 | tf_op jit(solution)/shard_map/ppermute | solution.py:19
  45.6 5.0 %fusion.24 = f32[2,16,8,5,256]{4,2,3,1,0:T(8,128)S(1)} fusion(bf16[3,3,3,256,256]{4,3,2,1,0:T(8,128)(2,1)S(1)} %copy-done, bf16[4,18,1,7,2,256]{5,3,4,1,0,2:T(8,128)(2,1)S(1)} %slice.56, bf16[4,18,1,8,5,256]{5,3,4,1,0,2:T(8,128)(2,1)S(1)} %copy.24, pred[8,5]{0,1:T(8,128)(4,1)S(1)} %copy-done.7), kind=kOutput, calls=%fused_computation.41 | convolution fusion | flops 4536369152 | bytes 6840360 | tf_op jit(solution)/shard_map/conv_general_dilated | solution.py:34
  54.3 2.4 copy.44
  58.9 2.3 copy.27
  61.2 110.0 %all-gather.2.cloned.1.call-done = bf16[4096,1024]{1,0:T(8,128)(2,1)} async-done(((bf16[256,1024]{1,0:T(8,128)(2,1)}), bf16[4096,1024]{1,0:T(8,128)(2,1)}) %all-gather.2.cloned.1.call-update) | async-done | bytes 8388624 | tf_op jit(solution)/shard_map/all_gather | solution.py:51
  171.1 10.0 %convolution_convert_fusion = bf16[4096,384]{1,0:T(8,128)(2,1)} fusion(bf16[4096,1024]{1,0:T(8,128)(2,1)} %all-gather.2.cloned.1.call-done, bf16[1024,384]{0,1:T(8,128)(2,1)} %bitcast.103), kind=kOutput, calls=%fused_computation.25 | convolution fusion | flops 3222798336 | bytes 12320768 | tf_op jit(solution)/shard_map/dot_general | solution.py:50
  181.2 9.0 %reshape.153 = bf16[4,4,2,8,16,1,3,128]{7,6,4,3,2,1,0,5:T(4,128)(2,1)} reshape(bf16[4096,384]{1,0:T(8,128)(2,1)} %convolution_convert_fusion) | data formatting | bytes 6291456 | tf_op jit(solution)/shard_map/reshape | solution.py:59
  190.2 3.1 %copy.28 = bf16[4,2,8,4,16,1,3,128]{7,4,3,6,2,1,0,5:T(8,128)(2,1)S(1)} copy(bf16[4,2,8,4,16,1,3,128]{7,6,4,2,1,3,0,5:T(4,128)(2,1)} %bitcast.95) | data formatting | bytes 6291456 | tf_op jit(solution)/shard_map/transpose | solution.py:62
  202.7 2.3 slice_bitcast_fusion.1
  205.0 3.4 %pad_maximum_fusion = bf16[8,16,64,1,256]{4,2,1,0,3:T(8,128)(2,1)} fusion(bf16[8,4,64,1,256]{4,2,1,0,3:T(8,128)(2,1)} %collective-permute-done.7, bf16[8,8,64,1,256]{4,2,1,0,3:T(8,128)(2,1)S(1)} %copy-done.3, bf16[8,4,64,1,256]{4,2,1,0,3:T(8,128)(2,1)} %collective-permute-done.6), kind=kLoop, calls=%fused_computation.26 | loop fusion | flops 4194304 | bytes 8388608 | tf_op jit(solution)/shard_map/concatenate | solution.py:15
  208.9 47.0 %while.12 = (s32[]{:T(128)}, bf16[2,8,4,64,1,128]{5,3,2,1,4,0:T(8,128)(2,1)}, s32[2]{0:T(128)}, bf16[8,16,64,1,256]{4,2,1,0,3:T(8,128)(2,1)}, s32[]{:T(128)}, /*...) while((s32[]{:T(128)}, ...), condition=%wide.region_4.5_spmd, body=%wide.region_1.4_spmd.sunk | while | flops 824439104 | bytes 54576908 | solution.py:94
  210.9 3.9 %fusion.50 = (f32[8,4,64]{2,1,0:T(4,128)S(1)}, f32[8,4,64,12,64]{2,4,3,1,0:T(8,128)S(1)}) fusion(pred[4,12]{1,0:T(4,128)(4,1)S(1)} %fusion.49, bf16[8,16,64,1,256]{4,2,1,0,3:T(8,128)(2,1)} %get-tuple-element.180, s32[]{:T(128)S(6)} %select_n.46, bf16[8,8,64,1,128]{4,2,1,0,3:T(8,128)(2,1)} %get-tuple-element.182, s32[]{:T(128)S(6)} %select_n.47), kind=kOutput, calls=%fused_computation.3.clone.1 | convolution fusion | flops 407369728 | bytes 8396856 | tf_op jit(solution)/shard_map/while/body/eval_jaxpr/tiahd,tjbhd->thiajb/dot_general | solution.py:78
  214.8 4.5 %copy-done.1 = f32[8,4,64,12,64]{2,4,3,1,0:T(8,128)} copy-done((f32[8,4,64,12,64]{2,4,3,1,0:T(8,128)}, f32[8,4,64,12,64]{2,4,3,1,0:T(8,128)S(1)}, u32[]{:S(2)}) %copy-start.1) | copy-done | bytes 6291480 | tf_op jit(solution)/shard_map/while
  219.3 4.0 %fusion.51 = f32[8,4,64]{2,1,0:T(4,128)} fusion(f32[8,4,64,12,64]{2,4,3,1,0:T(8,128)S(1)} %get-tuple-element.151, f32[8,4,64]{2,1,0:T(4,128)S(1)} %get-tuple-element.152, pred[4,12]{1,0:T(4,128)(4,1)S(1)} %fusion.49), kind=kLoop, calls=%fused_computation.4.clone.1 | loop fusion | flops 6289408 | bytes 6307888 | tf_op jit(solution)/shard_map/while/body/eval_jaxpr/reduce_sum | solution.py:88
  223.3 9.1 %fusion.52 = bf16[2,8,4,64,1,128]{5,3,2,1,4,0:T(8,128)(2,1)} fusion(bf16[2,8,4,64,1,128]{5,3,2,1,4,0:T(8,128)(2,1)} %get-tuple-element.166, s32[]{:T(128)} %get-tuple-element.165, f32[8,4,64,12,64]{2,4,3,1,0:T(8,128)} %copy-done.1, f32[8,4,64]{2,1,0:T(4,128)} %fusion.51, f32[8,4,64]{2,1,0:T(4,128)S(1)} %get-tuple-element.152, ...), kind=kOutput, calls=%fused_computation.12.clone.1 | convolution fusion | flops 410779648 | bytes 14705672 | tf_op jit(solution)/shard_map/while/body/eval_jaxpr/thiajb,tjbhd->tiahd/dot_general | solution.py:89
  234.4 3.9 %fusion.50 = (f32[8,4,64]{2,1,0:T(4,128)S(1)}, f32[8,4,64,12,64]{2,4,3,1,0:T(8,128)S(1)}) fusion(pred[4,12]{1,0:T(4,128)(4,1)S(1)} %fusion.49, bf16[8,16,64,1,256]{4,2,1,0,3:T(8,128)(2,1)} %get-tuple-element.180, s32[]{:T(128)S(6)} %select_n.46, bf16[8,8,64,1,128]{4,2,1,0,3:T(8,128)(2,1)} %get-tuple-element.182, s32[]{:T(128)S(6)} %select_n.47), kind=kOutput, calls=%fused_computation.3.clone.1 | convolution fusion | flops 407369728 | bytes 8396856 | tf_op jit(solution)/shard_map/while/body/eval_jaxpr/tiahd,tjbhd->thiajb/dot_general | solution.py:78
  238.3 4.5 %copy-done.1 = f32[8,4,64,12,64]{2,4,3,1,0:T(8,128)} copy-done((f32[8,4,64,12,64]{2,4,3,1,0:T(8,128)}, f32[8,4,64,12,64]{2,4,3,1,0:T(8,128)S(1)}, u32[]{:S(2)}) %copy-start.1) | copy-done | bytes 6291480 | tf_op jit(solution)/shard_map/while
  242.8 4.0 %fusion.51 = f32[8,4,64]{2,1,0:T(4,128)} fusion(f32[8,4,64,12,64]{2,4,3,1,0:T(8,128)S(1)} %get-tuple-element.151, f32[8,4,64]{2,1,0:T(4,128)S(1)} %get-tuple-element.152, pred[4,12]{1,0:T(4,128)(4,1)S(1)} %fusion.49), kind=kLoop, calls=%fused_computation.4.clone.1 | loop fusion | flops 6289408 | bytes 6307888 | tf_op jit(solution)/shard_map/while/body/eval_jaxpr/reduce_sum | solution.py:88
  246.8 9.1 %fusion.52 = bf16[2,8,4,64,1,128]{5,3,2,1,4,0:T(8,128)(2,1)} fusion(bf16[2,8,4,64,1,128]{5,3,2,1,4,0:T(8,128)(2,1)} %get-tuple-element.166, s32[]{:T(128)} %get-tuple-element.165, f32[8,4,64,12,64]{2,4,3,1,0:T(8,128)} %copy-done.1, f32[8,4,64]{2,1,0:T(4,128)} %fusion.51, f32[8,4,64]{2,1,0:T(4,128)S(1)} %get-tuple-element.152, ...), kind=kOutput, calls=%fused_computation.12.clone.1 | convolution fusion | flops 410779648 | bytes 14705672 | tf_op jit(solution)/shard_map/while/body/eval_jaxpr/thiajb,tjbhd->tiahd/dot_general | solution.py:89
  255.9 2.3 copy.30
  (59 shorter events, 32.2 us)
Async XLA Ops:
  7.2 38.5 %copy-start = (bf16[3,3,3,256,256]{4,3,2,1,0:T(8,128)(2,1)S(1)}, bf16[3,3,3,256,256]{4,3,2,1,0:T(8,128)(2,1)}, u32[]{:S(2)}) copy-start(bf16[3,3,3,256,256]{4,3,2,1,0:T(8,128)(2,1)} %param.8) | copy-start | bytes 10616836
  7.2 164.0 %all-gather.2.cloned.1.call-start = ((), (), s32[]{:S(2)}) async-start(), calls=%async_computation | async-start | bytes 8912896 | tf_op jit(solution)/shard_map/all_gather | solution.py:51
  10.4 10.4 %collective-permute-start = (bf16[1,16,32,256]{3,1,2,0:T(8,128)(2,1)S(1)}, bf16[1,16,32,256]{3,1,2,0:T(8,128)(2,1)S(1)}, u32[]{:S(2)}, u32[]{:S(2)}) collective-permute-start(bf16[1,16,32,256]{3,1,2,0:T(8,128)(2,1)S(1)} %get-tuple-element.106), channel_id=1, source_target_pairs={{0,8},{8,16},{16,24},{1,9},{9,17},{17,25},{2,10},{10,18},{18,26},{... | collective-permute-start | bytes 786440 | tf_op jit(solution)/shard_map/ppermute | solution.py:17
  15.3 13.1 %collective-permute-start.1 = (bf16[1,16,32,256]{3,1,2,0:T(8,128)(2,1)S(1)}, bf16[1,16,32,256]{3,1,2,0:T(8,128)(2,1)S(1)}, u32[]{:S(2)}, u32[]{:S(2)}) collective-permute-start(bf16[1,16,32,256]{3,1,2,0:T(8,128)(2,1)S(1)} %get-tuple-element.107), channel_id=1, source_target_pairs={{8,0},{16,8},{24,16},{9,1},{17,9},{25,17},{10,2},{18,10},{26,18},{... | collective-permute-start | bytes 786440 | tf_op jit(solution)/shard_map/ppermute | solution.py:19
  28.6 2.6 collective-permute-start.2
  29.9 3.2 %collective-permute-start.3 = (bf16[4,1,32,256]{3,1,2,0:T(2,128)(2,1)S(1)}, bf16[4,1,32,256]{3,1,2,0:T(2,128)(2,1)S(1)}, u32[]{:S(2)}, u32[]{:S(2)}) collective-permute-start(bf16[4,1,32,256]{3,1,2,0:T(2,128)(2,1)S(1)} %get-tuple-element.105), channel_id=1, source_target_pairs={{4,0},{5,1},{6,2},{7,3},{12,8},{13,9},{14,10},{15,11},{20,16},{21,... | collective-permute-start | bytes 196616 | tf_op jit(solution)/shard_map/ppermute | solution.py:19
  33.2 5.2 %collective-permute-start.4 = (bf16[4,18,1,256]{3,1,2,0:T(8,128)(2,1)S(1)}, bf16[4,18,1,256]{3,1,2,0:T(8,128)(2,1)S(1)}, u32[]{:S(2)}, u32[]{:S(2)}) collective-permute-start(bf16[4,18,1,256]{3,1,2,0:T(8,128)(2,1)S(1)} %get-tuple-element.102), channel_id=1, source_target_pairs={{0,1},{1,2},{2,3},{4,5},{5,6},{6,7},{8,9},{9,10},{10,11},{12,13},{... | collective-permute-start | bytes 110600 | tf_op jit(solution)/shard_map/ppermute | solution.py:17
  36.6 6.0 %collective-permute-start.5 = (bf16[4,18,1,256]{3,1,2,0:T(8,128)(2,1)S(1)}, bf16[4,18,1,256]{3,1,2,0:T(8,128)(2,1)S(1)}, u32[]{:S(2)}, u32[]{:S(2)}) collective-permute-start(bf16[4,18,1,256]{3,1,2,0:T(8,128)(2,1)S(1)} %get-tuple-element.103), channel_id=1, source_target_pairs={{1,0},{2,1},{3,2},{5,4},{6,5},{7,6},{9,8},{10,9},{11,10},{13,12},{... | collective-permute-start | bytes 110600 | tf_op jit(solution)/shard_map/ppermute | solution.py:19
  44.5 1.1 copy-start.7
  45.6 5.4 %copy-start.5 = (bf16[2,16,32,256]{3,2,1,0:T(8,128)(2,1)S(1)}, bf16[2,16,32,256]{3,2,1,0:T(8,128)(2,1)}, u32[]{:S(2)}) copy-start(bf16[2,16,32,256]{3,2,1,0:T(8,128)(2,1)} %param.6) | copy-start | bytes 1572868
  193.3 3.7 %copy-start.4 = (bf16[4,2,8,4,16,1,3,128]{7,4,3,6,2,1,0,5:T(8,128)(2,1)}, bf16[4,2,8,4,16,1,3,128]{7,4,3,6,2,1,0,5:T(8,128)(2,1)S(1)}, u32[]{:S(2)}) copy-start(bf16[4,2,8,4,16,1,3,128]{7,4,3,6,2,1,0,5:T(8,128)(2,1)S(1)} %copy.28) | copy-start | bytes 9437188
  193.7 1.7 copy-start.2
  196.9 8.0 %collective-permute-start.6 = (bf16[8,4,64,1,256]{4,2,1,0,3:T(8,128)(2,1)}, bf16[8,4,64,1,256]{4,2,1,0,3:T(8,128)(2,1)}, u32[]{:S(2)}, u32[]{:S(2)}) collective-permute-start(bf16[8,4,64,1,256]{4,2,1,0,3:T(8,128)(2,1)} %get-tuple-element.100), channel_id=1, source_target_pairs={{0,4},{1,5},{2,6},{3,7},{8,12},{9,13},{10,14},{11,15},{16,20},{17,... | collective-permute-start | bytes 3145736 | tf_op jit(solution)/shard_map/ppermute | solution.py:17
  199.2 5.8 %collective-permute-start.7 = (bf16[8,4,64,1,256]{4,2,1,0,3:T(8,128)(2,1)}, bf16[8,4,64,1,256]{4,2,1,0,3:T(8,128)(2,1)}, u32[]{:S(2)}, u32[]{:S(2)}) collective-permute-start(bf16[8,4,64,1,256]{4,2,1,0,3:T(8,128)(2,1)} %get-tuple-element.101), channel_id=1, source_target_pairs={{4,0},{5,1},{6,2},{7,3},{12,8},{13,9},{14,10},{15,11},{20,16},{21,... | collective-permute-start | bytes 3145736 | tf_op jit(solution)/shard_map/ppermute | solution.py:19
  200.5 4.5 %copy-start.3 = (bf16[8,8,64,1,256]{4,2,1,0,3:T(8,128)(2,1)S(1)}, bf16[8,8,64,1,256]{4,2,1,0,3:T(8,128)(2,1)}, u32[]{:S(2)}) copy-start(bf16[8,8,64,1,256]{4,2,1,0,3:T(8,128)(2,1)} %copy-done.2) | copy-start | bytes 6291460
  210.9 3.9 %copy-start.6 = (pred[4,12]{1,0:T(4,128)(4,1)}, pred[4,12]{1,0:T(4,128)(4,1)S(1)}, u32[]{:S(2)}) copy-start(pred[4,12]{1,0:T(4,128)(4,1)S(1)} %fusion.49) | copy-start | bytes 148 | tf_op jit(solution)/shard_map/while
  214.8 4.5 %copy-start.1 = (f32[8,4,64,12,64]{2,4,3,1,0:T(8,128)}, f32[8,4,64,12,64]{2,4,3,1,0:T(8,128)S(1)}, u32[]{:S(2)}) copy-start(f32[8,4,64,12,64]{2,4,3,1,0:T(8,128)S(1)} %get-tuple-element.151) | copy-start | bytes 18874372 | tf_op jit(solution)/shard_map/while
  234.4 3.9 %copy-start.6 = (pred[4,12]{1,0:T(4,128)(4,1)}, pred[4,12]{1,0:T(4,128)(4,1)S(1)}, u32[]{:S(2)}) copy-start(pred[4,12]{1,0:T(4,128)(4,1)S(1)} %fusion.49) | copy-start | bytes 148 | tf_op jit(solution)/shard_map/while
  238.3 4.5 %copy-start.1 = (f32[8,4,64,12,64]{2,4,3,1,0:T(8,128)}, f32[8,4,64,12,64]{2,4,3,1,0:T(8,128)S(1)}, u32[]{:S(2)}) copy-start(f32[8,4,64,12,64]{2,4,3,1,0:T(8,128)S(1)} %get-tuple-element.151) | copy-start | bytes 18874372 | tf_op jit(solution)/shard_map/while
Sparse Core Ops, SparseCore 0:
  59.0 112.1 all-gather.1
where the time goes:
time: 268 us; the launch traced here: 265 us
  waiting for transfers between devices  128 us (48%)
  local copies, waits for them, and re-layouts  45.6 us (17%)
  matrix products  41 us (15%)
  other arithmetic  17.2 us (6%)
  starting transfers between devices  17.1 us (6%)
  between operations  14.3 us (5%)
    all_gather x1, waiting for transfers between devices, local(): lax.all_gather(patches, ('ta', 'wa'), axis=0, tiled=True)  110 us
    dot_general x2, matrix products, attend(): jnp.einsum('thiajb,tjbhd->tiahd', probs, value_part, preferred_element_ty...  18.2 us
    ppermute x4, waiting for transfers between devices, extended(): lax.ppermute(head, axis, [((i + 1) % count, i) for i in range(ends)])  13.7 us
    ppermute x4, starting transfers between devices, extended(): lax.ppermute(tail, axis, [(i, (i + 1) % count) for i in range(ends)])  11.9 us
    dot_general x1, matrix products, local(): jnp.dot(lax.all_gather(patches, ('ta', 'wa'), axis=0, tiled=True), own_we...  10 us
    while x8, local copies, waits for them, and re-layouts  9.01 us
    reshape x1, local copies, waits for them, and re-layouts, local(): gathered.reshape(n_time, n_width, t_dev, rows_dev, cols_dev, head_dev, qk...  8.98 us
    reduce_sum x2, other arithmetic, attend(): jnp.sum(exp_scores, axis=(4, 5), keepdims=True)  8.05 us
  transfers between devices with their start and end apart: 9, of which 6 were waited for; matrix products, arithmetic and copies ran while one was open for 3% of the time, Pallas kernels for 0%

commit v1 on v0

v1 whole, which is shorter than its diff:
```python
import functools

import jax
import jax.numpy as jnp
from jax import lax
from jax.experimental import pallas as pl
from jax.experimental.pallas import tpu as pltpu
from jax.sharding import PartitionSpec as P

WIN = 4
CH = 8
MESH = pl.DeviceIdType.MESH
F32 = jnp.float32
BF16 = jnp.bfloat16


def kernel(n_t, n_h, n_w, normed, cols, latents, cw_hbm, w_hbm, out_block, out_att,
           pad_n, pad_c, cf, x3, cw, wg, fbuf, pat, q_buf, kv, bias, o_buf,
           loc_sem, halo_s, halo_r, w_s, w_r, ag_s, ag_r, kv_s, kv_r, at_s, at_r):
    t_dev, h_dev, w_dev, ch = latents.shape
    rows = h_dev // 2
    cols_dev = w_dev // 2
    hd = q_buf.shape[-1]
    pc = n_w * cols_dev
    cpt = h_dev // CH
    prow = CH // 2
    it, ih, iw = lax.axis_index("ta"), lax.axis_index("ha"), lax.axis_index("wa")
    has = {"t-": it > 0, "t+": it < n_t - 1, "h-": ih > 0, "h+": ih < n_h - 1,
           "w-": iw > 0, "w+": iw < n_w - 1}
    opp = {"-": "+", "+": "-"}
    dev = {"t-": {"ta": it - 1}, "t+": {"ta": it + 1}, "h-": {"ha": ih - 1}, "h+": {"ha": ih + 1},
           "w-": {"wa": iw - 1}, "w+": {"wa": iw + 1}}

    def rcopy(src, dst, ss, rs, device):
        return pltpu.make_async_remote_copy(
            src_ref=src, dst_ref=dst, send_sem=ss, recv_sem=rs, device_id=device, device_id_type=MESH)

    cw_copy = pltpu.make_async_copy(cw_hbm, cw, loc_sem.at[0])
    cw_copy.start()
    own_w = pltpu.make_async_copy(w_hbm, wg.at[it], loc_sem.at[1])
    own_w.start()

    bar = pltpu.get_barrier_semaphore()
    count = jnp.int32(n_t - 1)
    for side in ("h-", "h+", "w-", "w+"):
        count = count + has[side].astype(jnp.int32)

        @pl.when(has[side])
        def _():
            pl.semaphore_signal(bar, inc=1, device_id=dev[side], device_id_type=MESH)
    for d in range(1, n_t):
        pl.semaphore_signal(bar, inc=1, device_id={"ta": lax.rem(it + d, n_t)}, device_id_type=MESH)
    pl.semaphore_wait(bar, count)

    def halo(i, side, src, dst):
        c = rcopy(src, dst, halo_s.at[i], halo_r.at[i], dev[side])
        from_side = side[0] + opp[side[1]]

        def start():
            @pl.when(has[side])
            def _():
                c.start()

        def recv():
            @pl.when(has[from_side])
            def _():
                c.wait_recv()

        def sent():
            @pl.when(has[side])
            def _():
                c.wait_send()
        return start, recv, sent

    own = pl.ds(h_dev, h_dev)
    ph_w = [halo(0, "w-", cols.at[0], pad_c.at[1, pl.ds(1, t_dev), own]),
            halo(1, "w+", cols.at[1], pad_c.at[0, pl.ds(1, t_dev), own])]
    ph_t = [halo(2, "t-", normed.at[0], pad_n.at[t_dev + 1, pl.ds(1, h_dev)]),
            halo(3, "t+", normed.at[t_dev - 1], pad_n.at[0, pl.ds(1, h_dev)])]
    ph_wt = [halo(4, "t-", pad_c.at[:, 1, own], pad_c.at[:, t_dev + 1, own]),
             halo(5, "t+", pad_c.at[:, t_dev, own], pad_c.at[:, 0, own])]
    ph_h = [halo(6, "h-", pad_n.at[:, 1], pad_n.at[:, h_dev + 1]),
            halo(7, "h+", pad_n.at[:, h_dev], pad_n.at[:, 0]),
            halo(8, "h-", pad_c.at[:, :, own], pad_c.at[:, :, pl.ds(2 * h_dev, h_dev)]),
            halo(9, "h+", pad_c.at[:, :, own], pad_c.at[:, :, pl.ds(0, h_dev)])]
    for s in ph_w + ph_t:
        s[0]()

    for d in range(1, n_t):
        rcopy(w_hbm, wg.at[it], w_s.at[d], w_r.at[d], {"ta": lax.rem(it + d, n_t)}).start()

    def zero(cond, ref, idx, shape):
        @pl.when(cond)
        def _():
            ref[idx] = jnp.zeros(shape, ref.dtype)

    no = {k: jnp.logical_not(v) for k, v in has.items()}
    full = slice(None)
    for side, s in (("w-", 0), ("w+", 1)):
        zero(no[side], pad_c, (s, pl.ds(1, t_dev), own), (t_dev, h_dev, ch))
    for side, t in (("t-", 0), ("t+", t_dev + 1)):
        zero(no[side], pad_c, (full, t, own), (2, h_dev, ch))
        zero(no[side], pad_n, (t, pl.ds(1, h_dev)), (h_dev, w_dev, ch))
    for side, r, b in (("h-", 0, 0), ("h+", h_dev + 1, 2 * h_dev)):
        zero(no[side], pad_n, (full, r), (t_dev + 2, w_dev, ch))
        zero(no[side], pad_c, (full, full, pl.ds(b, h_dev)), (2, t_dev + 2, h_dev, ch))
        zero(no[side], kv, (full, pl.ds(0 if side == "h-" else rows + WIN, WIN)),
             (t_dev, WIN) + kv.shape[2:])
    pad_n[pl.ds(1, t_dev), pl.ds(1, h_dev)] = normed[...]

    total_rows = rows * n_h
    bs = (WIN * pc, 3 * WIN * pc)
    qr = lax.broadcasted_iota(jnp.int32, bs, 0) // pc
    kr = lax.broadcasted_iota(jnp.int32, bs, 1) // pc - WIN
    for b in range(rows // WIN):
        kg = ih * rows + b * WIN + kr
        ok = (jnp.abs(qr - kr) <= WIN) & (kg >= 0) & (kg < total_rows)
        bias[b] = jnp.where(ok, 0.0, -1e30).astype(F32)

    for s in ph_w:
        s[1]()
    for s in ph_wt:
        s[0]()
    for s in ph_t + ph_wt:
        s[1]()
    for s in ph_h:
        s[0]()
    for s in ph_h:
        s[1]()

    cf[...] = pad_c[...].astype(F32)
    edge = lax.broadcasted_iota(jnp.int32, (w_dev, ch), 0)

    @pl.loop(0, t_dev + 2)
    def _(t):
        for r in range(h_dev + 2):
            v16 = pad_n[t, r]
            v = v16.astype(F32)
            hr = pl.ds(h_dev - 1 + r, 1)
            left = jnp.where(edge == 0, cf[0, t, hr, :], pltpu.roll(v, 1, 0))
            right = jnp.where(edge == w_dev - 1, cf[1, t, hr, :], pltpu.roll(v, w_dev - 1, 0))
            x3[t, r, :, 0:ch] = left.astype(BF16)
            x3[t, r, :, ch:2 * ch] = v16
            x3[t, r, :, 2 * ch:3 * ch] = right.astype(BF16)

    cw_copy.wait()

    def piece(src, t, i0):
        return pat.at[src, t, pl.ds(i0, prow)]

    sides = (("w+", 0), ("w-", 1))

    @pl.loop(0, t_dev * cpt)
    def _(c):
        t = c // cpt
        h0 = (c % cpt) * CH
        acc = latents[t, pl.ds(h0, CH)].astype(F32).reshape(CH * w_dev, ch)
        for a in range(3):
            for b in range(3):
                acc = acc + jnp.dot(
                    x3[t + a, pl.ds(h0 + b, CH)].reshape(CH * w_dev, 3 * ch), cw[a, b],
                    preferred_element_type=F32)
        blk = acc.astype(BF16)
        out_block[t, pl.ds(h0, CH)] = blk.reshape(CH, w_dev, ch)
        blk = blk.astype(F32)
        for k in range(ch // 128):
            fbuf[k] = blk[:, k * 128:(k + 1) * 128]
        for k in range(ch // 128):
            for dw in range(2):
                part = fbuf[k, pl.ds(dw, CH * cols_dev, stride=2), :].astype(BF16)
                part = part.reshape(prow, 2, cols_dev, 128)
                for dh in range(2):
                    lo = (dh * 2 + dw) * ch + k * 128
                    pat[iw, t, pl.ds((c % cpt) * prow, prow), :, lo:lo + 128] = part[:, dh]
        p = piece(iw, t, (c % cpt) * prow)
        for side, i in sides:
            @pl.when(has[side])
            def _():
                rcopy(p, p, ag_s.at[i, 0, c], ag_r.at[i, 0, c], dev[side]).start()

    def relay(t, d):
        for j in range(cpt):
            c = t * cpt + j
            for side, i in sides:
                src = iw - d if i == 0 else iw + d
                here = src >= 0 if i == 0 else src < n_w
                p = piece(src, t, j * prow)

                @pl.when(here)
                def _():
                    rcopy(p, p, ag_s.at[i, d - 1, c], ag_r.at[i, d - 1, c], dev[side]).wait_recv()
                    if d < n_w - 1:
                        @pl.when(has[side])
                        def _():
                            rcopy(p, p, ag_s.at[i, d, c], ag_r.at[i, d, c], dev[side]).start()

    def qkv(t):
        @pl.loop(0, n_t)
        def _(a):
            x = pat[:, t].reshape(n_w * rows * cols_dev, 4 * ch)
            y = jnp.dot(x, wg[a], preferred_element_type=F32).astype(BF16)
            y = y.reshape(n_w, rows, cols_dev, 3 * hd)
            for s in range(n_w):
                cc = pl.ds(s * cols_dev, cols_dev)
                q_buf[t, a, :, cc, :] = y[s, :, :, 0:hd]
                kv[t, pl.ds(WIN, rows), 2 * a, cc, :] = y[s, :, :, hd:2 * hd]
                kv[t, pl.ds(WIN, rows), 2 * a + 1, cc, :] = y[s, :, :, 2 * hd:3 * hd]

    def rim(t):
        return [("h-", rcopy(kv.at[t, pl.ds(WIN, WIN)], kv.at[t, pl.ds(rows + WIN, WIN)],
                             kv_s.at[t, 0], kv_r.at[t, 0], dev["h-"])),
                ("h+", rcopy(kv.at[t, pl.ds(rows, WIN)], kv.at[t, pl.ds(0, WIN)],
                             kv_s.at[t, 1], kv_r.at[t, 1], dev["h+"]))]

    scale = hd ** (-0.5) * 1.4426950408889634

    def attend(t):
        @pl.loop(0, n_t)
        def _(a):
            for b in range(rows // WIN):
                r = pl.ds(b * WIN, WIN)
                kr_ = pl.ds(b * WIN, 3 * WIN)
                q = q_buf[t, a, r].reshape(WIN * pc, hd)
                k = kv[t, kr_, 2 * a].reshape(3 * WIN * pc, hd)
                v = kv[t, kr_, 2 * a + 1].reshape(3 * WIN * pc, hd)
                s = lax.dot_general(q, k, (((1,), (1,)), ((), ())), preferred_element_type=F32)
                s = s + bias[b]
                m = jnp.max(s, axis=1, keepdims=True)
                e = jnp.exp2((s - m) * scale)
                z = jnp.sum(e, axis=1, keepdims=True)
                o = jnp.dot(e.astype(BF16), v, preferred_element_type=F32) / z
                o_buf[t, a, r] = o.astype(BF16).reshape(WIN, pc, hd)
            dst = out_att.at[it * t_dev + t]

            @pl.when(a != it)
            def _():
                rcopy(o_buf.at[t, a], dst, at_s.at[t, a], at_r.at[t, it], {"ta": a}).start()

            @pl.when(a == it)
            def _():
                pltpu.make_async_copy(o_buf.at[t, a], dst, loc_sem.at[2 + t]).start()

    def weights_in():
        own_w.wait()
        for d in range(1, n_t):
            src = lax.rem(it + n_t - d, n_t)
            rcopy(w_hbm, wg.at[src], w_s.at[d], w_r.at[d], {"ta": src}).wait_recv()

    for d in range(1, n_w):
        relay(0, d)
    weights_in()
    for t in range(t_dev):
        qkv(t)
        for side, c in rim(t):
            @pl.when(has[side])
            def _():
                c.start()
        if t + 1 < t_dev:
            for d in range(1, n_w):
                relay(t + 1, d)
        for side, c in rim(t):
            @pl.when(has[side[0] + opp[side[1]]])
            def _():
                c.wait_recv()
        attend(t)

    for t in range(t_dev):
        pltpu.make_async_copy(o_buf.at[t, it], out_att.at[it * t_dev + t], loc_sem.at[2 + t]).wait()
        for d in range(1, n_t):
            src = lax.rem(it + d, n_t)
            rcopy(o_buf.at[t, src], out_att.at[src * t_dev + t], at_s.at[t, src], at_r.at[t, src],
                  {"ta": src}).wait()
        for side, c in rim(t):
            @pl.when(has[side])
            def _():
                c.wait_send()
    for s in ph_w + ph_t + ph_wt + ph_h:
        s[2]()
    for d in range(1, n_t):
        rcopy(w_hbm, wg.at[it], w_s.at[d], w_r.at[d], {"ta": lax.rem(it + d, n_t)}).wait_send()
    for t in range(t_dev):
        for j in range(cpt):
            c = t * cpt + j
            for side, i in sides:
                for d in range(n_w - 1):
                    src = iw - d if i == 0 else iw + d
                    here = src >= 0 if i == 0 else src < n_w
                    p = piece(src, t, j * prow)

                    @pl.when(here & has[side])
                    def _():
                        rcopy(p, p, ag_s.at[i, d, c], ag_r.at[i, d, c], dev[side]).wait_send()


def local(latents, norm_gain, conv_weight, qkv_weight):
    n_t, n_h, n_w = (lax.axis_size(a) for a in ("ta", "ha", "wa"))
    t_dev, h_dev, w_dev, ch = latents.shape
    rows, cols_dev = h_dev // 2, w_dev // 2
    pd, head_dev, qkv_count, hd = qkv_weight.shape
    pc = n_w * cols_dev
    x = latents.astype(F32)
    rms = lax.rsqrt(jnp.mean(x * x, axis=-1, keepdims=True) + 1e-06)
    normed = jax.nn.silu(x * rms * norm_gain).astype(BF16)
    cols = jnp.stack([normed[:, :, 0], normed[:, :, w_dev - 1]])
    cw = conv_weight.reshape(3, 3, 3 * ch, ch)
    w2 = qkv_weight.reshape(pd, qkv_count * hd)
    frames = n_t * t_dev
    chunks = t_dev * (h_dev // CH)
    vm = pl.BlockSpec(memory_space=pltpu.VMEM)
    hbm = pl.BlockSpec(memory_space=pl.ANY)
    dma = pltpu.SemaphoreType.DMA
    block_out, att = pl.pallas_call(
        functools.partial(kernel, n_t, n_h, n_w),
        out_shape=(jax.ShapeDtypeStruct(latents.shape, BF16),
                   jax.ShapeDtypeStruct((frames, rows, pc, hd), BF16)),
        in_specs=[vm, vm, vm, hbm, hbm],
        out_specs=(vm, hbm),
        scratch_shapes=[
            pltpu.VMEM((t_dev + 2, h_dev + 2, w_dev, ch), BF16),
            pltpu.VMEM((2, t_dev + 2, 3 * h_dev, ch), BF16),
            pltpu.VMEM((2, t_dev + 2, 3 * h_dev, ch), F32),
            pltpu.VMEM((t_dev + 2, h_dev + 2, w_dev, 3 * ch), BF16),
            pltpu.VMEM((3, 3, 3 * ch, ch), BF16),
            pltpu.VMEM((n_t, pd, qkv_count * hd), BF16),
            pltpu.VMEM((ch // 128, CH * w_dev, 128), F32),
            pltpu.VMEM((n_w, t_dev, rows, cols_dev, pd), BF16),
            pltpu.VMEM((t_dev, n_t, rows, pc, hd), BF16),
            pltpu.VMEM((t_dev, rows + 2 * WIN, 2 * n_t, pc, hd), BF16),
            pltpu.VMEM((rows // WIN, WIN * pc, 3 * WIN * pc), F32),
            pltpu.VMEM((t_dev, n_t, rows, pc, hd), BF16),
            dma((2 + t_dev,)),
            dma((10,)), dma((10,)),
            dma((n_t,)), dma((n_t,)),
            dma((2, n_w, chunks)), dma((2, n_w, chunks)),
            dma((t_dev, 2)), dma((t_dev, 2)),
            dma((t_dev, n_t)), dma((t_dev, n_t)),
        ],
        compiler_params=pltpu.CompilerParams(
            collective_id=0, has_side_effects=True, vmem_limit_bytes=48 * 1024 * 1024),
    )(normed, cols, latents, cw, w2)
    return block_out, att.reshape(frames, rows, pc, head_dev, hd)


def solution(mesh):
    return jax.shard_map(
        local,
        mesh=mesh,
        in_specs=(P("ta", "ha", "wa", None), P(), P(), P(None, ("ta", "wa"), None, None)),
        out_specs=(P("ta", "ha", "wa", None), P(None, "ha", None, ("ta", "wa"), None)),
        check_vma=False,
    )
```

time: 268 us -> 117 us (0.44)
  waiting for transfers between devices: 128 us -> 0 us
  Pallas kernels: 0 us -> 108 us
  local copies, waits for them, and re-layouts: 45.6 us -> 3.99 us
  matrix products: 41 us -> 0 us
  starting transfers between devices: 17.1 us -> 0 us
  other arithmetic: 17.2 us -> 3.04 us
  between operations: 14.3 us -> 0.71 us
    all_gather x1 -> x0, waiting for transfers between devices: 110 us -> none  [local(): lax.all_gather(patches, ('ta', 'wa'), axis=0, tiled=True)]
    pallas_call x0 -> x1, Pallas kernels: none -> 108 us  [local(): pl.pallas_call(functools.partial(kernel, n_t, n_h, n_w), out_shape=(jax.S...]
    dot_general x5 -> x0, matrix products: 36 us -> none  [the longest x2 18.2 us: attend(): jnp.einsum('thiajb,tjbhd->tiahd', probs, value_part, preferred_element_ty...]
    ppermute x8 -> x0, waiting for transfers between devices: 18.4 us -> none  [the longest x4 13.7 us: extended(): lax.ppermute(head, axis, [((i + 1) % count, i) for i in range(ends)])]
    ppermute x8 -> x0, starting transfers between devices: 17.1 us -> none  [the longest x4 11.9 us: extended(): lax.ppermute(tail, axis, [(i, (i + 1) % count) for i in range(ends)])]
    reshape x5 -> x1, local copies, waits for them, and re-layouts: 16 us -> 0.35 us  [local(): w2 = qkv_weight.reshape(pd, qkv_count * hd)]
    while x8 -> x0, local copies, waits for them, and re-layouts: 9.01 us -> none
    reduce_sum x3 -> x1, other arithmetic: 9.6 us -> 1.48 us  [local(): rms = lax.rsqrt(jnp.mean(x * x, axis=-1, keepdims=True) + 1e-06)]
  transfers between devices with their start and end apart: 9 -> 0, of which waited for: 6 -> 0; matrix products, arithmetic and copies ran while one was open for 3% -> 0% of each run, Pallas kernels for 0% -> 0%
where the time goes in v1:
time: 117 us; the launch traced here: 116 us
  Pallas kernels  108 us (92%)
  local copies, waits for them, and re-layouts  3.99 us (3%)
  other arithmetic  3.04 us (3%)
    pallas_call x1, Pallas kernels, local(): pl.pallas_call(functools.partial(kernel, n_t, n_h, n_w), out_shape=(jax.S...  108 us
    unnamed x5, local copies, waits for them, and re-layouts  3.18 us

profile of v1, /device:TPU:0, one launch (start us, length us, event | category | flops | bytes accessed | tf_op | source)
XLA Modules:
  0.0 116.0 jit_solution(12855590961279752538)
XLA Ops:
  0.6 0.0 copy-start
  0.6 1.5 %fusion = f32[2,16,32]{1,0,2:T(2,128)S(1)} fusion(bf16[2,16,32,256]{3,2,1,0:T(8,128)(2,1)} %latents.1), kind=kLoop, calls=%fused_computation.2 | loop fusion | flops 785408 | bytes 528384 | tf_op jit(solution)/shard_map/reduce_sum | solution.py:302
  2.1 0.1 copy.22
  2.2 0.1 copy.23
  2.3 1.5 %fusion.7 = bf16[2,16,32,256]{3,1,0,2:T(8,128)(2,1)S(1)} fusion(f32[256]{0:T(256)} %param.5, f32[2,16,32]{1,0,2:T(2,128)S(1)} %copy.23, bf16[2,16,32,256]{3,2,1,0:T(8,128)(2,1)} %latents.1), kind=kLoop, calls=%fused_computation.9 | loop fusion | flops 2097152 | bytes 1053696 | tf_op jit(solution)/shard_map/convert_element_type | solution.py:303
  3.9 0.3 copy.25.normed
  4.2 1.4 %copy.24 = bf16[1024,1,3,128]{0,3,2,1:T(8,128)(2,1)S(1)} copy(bf16[1024,1,3,128]{3,0,2,1:T(8,128)(2,1)} %param.7) | data formatting | bytes 1572864 | tf_op args[3]
  5.6 0.4 copy.26.w_hbm
  6.0 0.0 copy-done
  6.0 108.3 %shard_map.59 = (bf16[2,16,32,256]{3,2,1,0:T(8,128)(2,1)S(1)}, bf16[8,8,64,128]{3,2,1,0:T(8,128)(2,1)S(1)}) custom-call(bf16[2,16,32,256]{3,2,1,0:T(8,128)(2,1)S(1)} %copy.25.normed, bf16[2,2,16,256]{3,2,1,0:T(8,128)(2,1)S(1)} %pad_maximum_fusion.cols, bf16[2,16,32,256]{3,2,1,0:T(8,128)(2,1)S(1)} %copy-done, bf16[3,3,768,256]{3,2,1,0:T(8,128)(2,1)} %bitcast.10, ...), custom_call_target="tpu_custom_call" | custom-call | tf_op jit(solution)/shard_map/pallas_call | solution.py:312
  114.3 0.8 copy.32
  115.0 1.0 copy.33
  (3 shorter events, 0.0 us)
Async XLA Ops:
  0.6 5.3 %copy-start = (bf16[2,16,32,256]{3,2,1,0:T(8,128)(2,1)S(1)}, bf16[2,16,32,256]{3,2,1,0:T(8,128)(2,1)}, u32[]{:S(2)}) copy-start(bf16[2,16,32,256]{3,2,1,0:T(8,128)(2,1)} %latents.1) | copy-start | bytes 1572868

commit v2 on v1

v2 whole, which is shorter than its diff:
```python
import functools

import jax
import jax.numpy as jnp
from jax import lax
from jax.experimental import pallas as pl
from jax.experimental.pallas import tpu as pltpu
from jax.sharding import PartitionSpec as P

WIN = 4
CH = 8
MESH = pl.DeviceIdType.MESH
F32 = jnp.float32
BF16 = jnp.bfloat16


def kernel(n_t, n_h, n_w, latents, gain, cw_hbm, w_hbm, out_block, out_att,
           pad_n, edge_f, edge_b, pad_c, cf, x3, acc_buf, cw, wg, fbuf, pat, q_buf, kv, bias, o_buf,
           loc_sem, halo_s, halo_r, w_s, w_r, wf_s, wf_r, ag_s, ag_r, kv_s, kv_r, at_s, at_r):
    t_dev, h_dev, w_dev, ch = latents.shape
    rows = h_dev // 2
    cols_dev = w_dev // 2
    hd = q_buf.shape[-1]
    pd = pat.shape[-1]
    pc = n_w * cols_dev
    cpt = h_dev // CH
    prow = CH // 2
    it, ih, iw = lax.axis_index("ta"), lax.axis_index("ha"), lax.axis_index("wa")
    has = {"t-": it > 0, "t+": it < n_t - 1, "h-": ih > 0, "h+": ih < n_h - 1,
           "w-": iw > 0, "w+": iw < n_w - 1}
    opp = {"-": "+", "+": "-"}
    dev = {"t-": {"ta": it - 1}, "t+": {"ta": it + 1}, "h-": {"ha": ih - 1}, "h+": {"ha": ih + 1},
           "w-": {"wa": iw - 1}, "w+": {"wa": iw + 1}}

    def rcopy(src, dst, ss, rs, device):
        return pltpu.make_async_remote_copy(
            src_ref=src, dst_ref=dst, send_sem=ss, recv_sem=rs, device_id=device, device_id_type=MESH)

    cw_copy = pltpu.make_async_copy(cw_hbm, cw, loc_sem.at[0])
    cw_copy.start()
    own_w = pltpu.make_async_copy(w_hbm, wg.at[it], loc_sem.at[1])
    own_w.start()

    bar = pltpu.get_barrier_semaphore()
    count = jnp.int32(n_t - 1)
    for side in ("h-", "h+", "w-", "w+"):
        count = count + has[side].astype(jnp.int32)

        @pl.when(has[side])
        def _():
            pl.semaphore_signal(bar, inc=1, device_id=dev[side], device_id_type=MESH)
    for d in range(1, n_t):
        pl.semaphore_signal(bar, inc=1, device_id={"ta": lax.rem(it + d, n_t)}, device_id_type=MESH)

    @pl.loop(0, t_dev)
    def _(t):
        for r in range(h_dev):
            x = latents[t, r].astype(F32)
            ms = jnp.sum(x * x, axis=-1, keepdims=True) * (1.0 / ch)
            n = x * lax.rsqrt(ms + 1e-06) * gain[...]
            n = n / (1.0 + jnp.exp(-n))
            pad_n[t + 1, r + 1] = n.astype(BF16)
            edge_f[0, t, r:r + 1, :] = n[0:1]
            edge_f[1, t, r:r + 1, :] = n[w_dev - 1:w_dev]

    edge_b[...] = edge_f[...].astype(BF16)
    pl.semaphore_wait(bar, count)

    def halo(i, side, src, dst):
        c = rcopy(src, dst, halo_s.at[i], halo_r.at[i], dev[side])
        from_side = side[0] + opp[side[1]]

        def start():
            @pl.when(has[side])
            def _():
                c.start()

        def recv():
            @pl.when(has[from_side])
            def _():
                c.wait_recv()

        def sent():
            @pl.when(has[side])
            def _():
                c.wait_send()
        return start, recv, sent

    own = pl.ds(h_dev, h_dev)
    low = pl.ds(0, h_dev)
    high = pl.ds(2 * h_dev, h_dev)
    own_t = pl.ds(1, t_dev)
    own_h = pl.ds(1, h_dev)
    ph_w = [halo(0, "w-", edge_b.at[0], pad_c.at[1, own_t, own]),
            halo(1, "w+", edge_b.at[1], pad_c.at[0, own_t, own])]
    ph_t = {"t+": halo(2, "t-", pad_n.at[1, own_h], pad_n.at[t_dev + 1, own_h]),
            "t-": halo(3, "t+", pad_n.at[t_dev, own_h], pad_n.at[0, own_h])}
    ph_wt = {"t+": halo(4, "t-", pad_c.at[:, 1, own], pad_c.at[:, t_dev + 1, own]),
             "t-": halo(5, "t+", pad_c.at[:, t_dev, own], pad_c.at[:, 0, own])}

    def rows_cols(i, ts):
        return ([halo(i, "h-", pad_n.at[ts, 1], pad_n.at[ts, h_dev + 1]),
                 halo(i + 1, "h+", pad_n.at[ts, h_dev], pad_n.at[ts, 0])],
                [halo(i + 2, "h-", pad_c.at[:, ts, own], pad_c.at[:, ts, high]),
                 halo(i + 3, "h+", pad_c.at[:, ts, own], pad_c.at[:, ts, low])])

    hr_own, hc_own = rows_cols(6, own_t)
    ph_h = {"t-": rows_cols(10, pl.ds(0, 1)), "t+": rows_cols(14, pl.ds(t_dev + 1, 1))}
    for s in list(ph_t.values()) + ph_w + hr_own:
        s[0]()

    def zero(cond, ref, idx, shape):
        @pl.when(cond)
        def _():
            ref[idx] = jnp.zeros(shape, ref.dtype)

    no = {k: jnp.logical_not(v) for k, v in has.items()}
    full = slice(None)
    for side, s in (("w-", 0), ("w+", 1)):
        zero(no[side], pad_c, (s, own_t, own), (t_dev, h_dev, ch))
    for side, t in (("t-", 0), ("t+", t_dev + 1)):
        zero(no[side], pad_c, (full, t, own), (2, h_dev, ch))
        zero(no[side], pad_n, (t, own_h), (h_dev, w_dev, ch))
    for side, r, b in (("h-", 0, low), ("h+", h_dev + 1, high)):
        zero(no[side], pad_n, (full, r), (t_dev + 2, w_dev, ch))
        zero(no[side], pad_c, (full, full, b), (2, t_dev + 2, h_dev, ch))
        zero(no[side], kv, (full, pl.ds(0 if side == "h-" else rows + WIN, WIN)),
             (t_dev, WIN) + kv.shape[2:])

    for s in ph_w:
        s[1]()
    for s in list(ph_wt.values()) + hc_own:
        s[0]()

    edge = lax.broadcasted_iota(jnp.int32, (w_dev, ch), 0)

    def build(t, r):
        v16 = pad_n[t, r]
        v = v16.astype(F32)
        hr = pl.ds(h_dev - 1 + r, 1)
        left = jnp.where(edge == 0, cf[0, t, hr, :], pltpu.roll(v, 1, 0))
        right = jnp.where(edge == w_dev - 1, cf[1, t, hr, :], pltpu.roll(v, w_dev - 1, 0))
        x3[t, r, :, 0:ch] = left.astype(BF16)
        x3[t, r, :, ch:2 * ch] = v16
        x3[t, r, :, 2 * ch:3 * ch] = right.astype(BF16)

    cf[:, own_t, own] = pad_c[:, own_t, own].astype(F32)

    @pl.loop(1, t_dev + 1)
    def _(t):
        for r in range(1, h_dev + 1):
            build(t, r)

    for s in hr_own + hc_own:
        s[1]()
    for b in (low, high):
        cf[:, own_t, b] = pad_c[:, own_t, b].astype(F32)

    @pl.loop(1, t_dev + 1)
    def _(t):
        for r in (0, h_dev + 1):
            build(t, r)

    cw_copy.wait()

    def taps(acc, t, h0, frames):
        for a in frames:
            for b in range(3):
                acc = acc + jnp.dot(
                    x3[t + a, pl.ds(h0 + b, CH)].reshape(CH * w_dev, 3 * ch), cw[a, b],
                    preferred_element_type=F32)
        return acc

    for t in range(t_dev):
        @pl.loop(0, cpt)
        def _(j):
            acc = latents[t, pl.ds(j * CH, CH)].astype(F32).reshape(CH * w_dev, ch)
            acc_buf[t, j] = taps(acc, t, j * CH, [a for a in range(3) if 1 <= t + a <= t_dev])

    def halo_frame(side):
        ph_t[side][1]()
        ph_wt[side][1]()
        hs = ph_h[side][0] + ph_h[side][1]
        for s in hs:
            s[0]()
        f = 0 if side == "t-" else t_dev + 1
        cf[:, f, own] = pad_c[:, f, own].astype(F32)
        for r in range(1, h_dev + 1):
            build(f, r)
        for s in hs:
            s[1]()
        for b in (low, high):
            cf[:, f, b] = pad_c[:, f, b].astype(F32)
        for r in (0, h_dev + 1):
            build(f, r)

    def finish(t):
        @pl.loop(0, cpt)
        def _(j):
            h0 = j * CH
            blk = taps(acc_buf[t, j], t, h0, [a for a in range(3) if not 1 <= t + a <= t_dev])
            blk = blk.astype(BF16)
            out_block[t, pl.ds(h0, CH)] = blk.reshape(CH, w_dev, ch)
            blk = blk.astype(F32)
            for k in range(ch // 128):
                fbuf[k] = blk[:, k * 128:(k + 1) * 128]
            for k in range(ch // 128):
                for dw in range(2):
                    part = fbuf[k, pl.ds(dw, CH * cols_dev, stride=2), :].astype(BF16)
                    part = part.reshape(prow, 2, cols_dev, 128)
                    for dh in range(2):
                        lo = (dh * 2 + dw) * ch + k * 128
                        pat[iw, t, pl.ds(j * prow, prow), :, lo:lo + 128] = part[:, dh]

    def piece(src, t, i0):
        return pat.at[src, t, pl.ds(i0, prow)]

    sides = (("w+", 0), ("w-", 1))

    def send_own(t):
        for j in range(cpt):
            c = t * cpt + j
            p = piece(iw, t, j * prow)
            for side, i in sides:
                @pl.when(has[side])
                def _():
                    rcopy(p, p, ag_s.at[i, 0, c], ag_r.at[i, 0, c], dev[side]).start()

    def relay(t, d):
        for j in range(cpt):
            c = t * cpt + j
            for side, i in sides:
                src = iw - d if i == 0 else iw + d
                here = src >= 0 if i == 0 else src < n_w
                p = piece(src, t, j * prow)

                @pl.when(here)
                def _():
                    rcopy(p, p, ag_s.at[i, d - 1, c], ag_r.at[i, d - 1, c], dev[side]).wait_recv()
                    if d < n_w - 1:
                        @pl.when(has[side])
                        def _():
                            rcopy(p, p, ag_s.at[i, d, c], ag_r.at[i, d, c], dev[side]).start()

    pair = n_h % 2 == 0
    part_rows = pd // 2 if pair else pd
    mine = pl.ds((ih % 2) * part_rows, part_rows) if pair else pl.ds(0, pd)
    other = {"ha": ih + 1 - 2 * (ih % 2)}
    theirs = pl.ds((1 - ih % 2) * part_rows, part_rows) if pair else None

    def w_copy(d, src):
        return rcopy(w_hbm.at[:, mine], wg.at[src, :, mine], w_s.at[d], w_r.at[d],
                     {"ta": lax.rem(it + d, n_t)})

    def w_hand(d, part):
        src = lax.rem(it + n_t - d, n_t)
        return rcopy(wg.at[src, :, part], wg.at[src, :, part], wf_s.at[d], wf_r.at[d], other)

    def w_start():
        for d in range(1, n_t):
            w_copy(d, it).start()

    def w_mid():
        for d in range(1, n_t):
            w_copy(d, lax.rem(it + n_t - d, n_t)).wait_recv()
            if pair:
                w_hand(d, mine).start()

    def w_end():
        own_w.wait()
        if pair:
            for d in range(1, n_t):
                w_hand(d, theirs).wait_recv()

    def qkv(t):
        @pl.loop(0, n_t)
        def _(a):
            x = pat[:, t].reshape(n_w * rows * cols_dev, pd)
            w = jnp.concatenate([wg[a, s] for s in range(3)], axis=1)
            y = jnp.dot(x, w, preferred_element_type=F32).astype(BF16)
            y = y.reshape(n_w, rows, cols_dev, 3 * hd)
            for s in range(n_w):
                cc = pl.ds(s * cols_dev, cols_dev)
                q_buf[t, a, :, cc, :] = y[s, :, :, 0:hd]
                kv[t, pl.ds(WIN, rows), 2 * a, cc, :] = y[s, :, :, hd:2 * hd]
                kv[t, pl.ds(WIN, rows), 2 * a + 1, cc, :] = y[s, :, :, 2 * hd:3 * hd]

    def rim(t):
        return [halo_kv(t, 0, "h-", kv.at[t, pl.ds(WIN, WIN)], kv.at[t, pl.ds(rows + WIN, WIN)]),
                halo_kv(t, 1, "h+", kv.at[t, pl.ds(rows, WIN)], kv.at[t, pl.ds(0, WIN)])]

    def halo_kv(t, i, side, src, dst):
        c = rcopy(src, dst, kv_s.at[t, i], kv_r.at[t, i], dev[side])
        return has[side], has[side[0] + opp[side[1]]], c

    def rim_start(t):
        for out, _, c in rim(t):
            @pl.when(out)
            def _():
                c.start()

    def rim_recv(t):
        for _, inn, c in rim(t):
            @pl.when(inn)
            def _():
                c.wait_recv()

    scale = hd ** (-0.5) * 1.4426950408889634

    def attend(t, lo, hi):
        @pl.loop(lo, hi)
        def _(step):
            a = lax.rem(it + 1 + step, n_t)
            for b in range(rows // WIN):
                r = pl.ds(b * WIN, WIN)
                kr_ = pl.ds(b * WIN, 3 * WIN)
                q = q_buf[t, a, r].reshape(WIN * pc, hd)
                k = kv[t, kr_, 2 * a].reshape(3 * WIN * pc, hd)
                v = kv[t, kr_, 2 * a + 1].reshape(3 * WIN * pc, hd)
                s = lax.dot_general(q, k, (((1,), (1,)), ((), ())), preferred_element_type=F32)
                s = s + bias[b]
                m = jnp.max(s, axis=1, keepdims=True)
                e = jnp.exp2((s - m) * scale)
                z = jnp.sum(e, axis=1, keepdims=True)
                o = jnp.dot(e.astype(BF16), v, preferred_element_type=F32) / z
                o_buf[t, a, r] = o.astype(BF16).reshape(WIN, pc, hd)
            dst = out_att.at[it * t_dev + t]

            @pl.when(a != it)
            def _():
                rcopy(o_buf.at[t, a], dst, at_s.at[t, a], at_r.at[t, it], {"ta": a}).start()

            @pl.when(a == it)
            def _():
                pltpu.make_async_copy(o_buf.at[t, a], dst, loc_sem.at[2 + t]).start()

    halo_frame("t-")
    if t_dev == 1:
        halo_frame("t+")
    finish(0)
    send_own(0)
    for t in range(1, t_dev):
        if t == t_dev - 1:
            halo_frame("t+")
        finish(t)
    w_start()

    total_rows = rows * n_h
    bs = (WIN * pc, 3 * WIN * pc)
    qr = lax.broadcasted_iota(jnp.int32, bs, 0) // pc
    kr = lax.broadcasted_iota(jnp.int32, bs, 1) // pc - WIN
    for b in range(rows // WIN):
        kg = ih * rows + b * WIN + kr
        ok = (jnp.abs(qr - kr) <= WIN) & (kg >= 0) & (kg < total_rows)
        bias[b] = jnp.where(ok, 0.0, -1e30).astype(F32)

    for d in range(1, n_w - 1):
        relay(0, d)
    if t_dev > 1:
        send_own(1)
    w_mid()
    if n_w > 1:
        relay(0, n_w - 1)
    w_end()
    for t in range(t_dev):
        more = t + 1 < t_dev
        qkv(t)
        rim_start(t)
        steps = n_w - 2
        rim_done = False
        for d in range(1, n_w - 1):
            if more:
                relay(t + 1, d)
            if not rim_done:
                rim_recv(t)
                rim_done = True
            attend(t, n_t * (d - 1) // steps, n_t * d // steps)
        if not rim_done:
            rim_recv(t)
            attend(t, 0, n_t)
        if more:
            if t + 2 < t_dev:
                send_own(t + 2)
            if n_w > 1:
                relay(t + 1, n_w - 1)

    for t in range(t_dev):
        pltpu.make_async_copy(o_buf.at[t, it], out_att.at[it * t_dev + t], loc_sem.at[2 + t]).wait()
        for d in range(1, n_t):
            src = lax.rem(it + d, n_t)
            rcopy(o_buf.at[t, src], out_att.at[src * t_dev + t], at_s.at[t, src], at_r.at[t, src],
                  {"ta": src}).wait()
        for out, _, c in rim(t):
            @pl.when(out)
            def _():
                c.wait_send()
    for s in (ph_w + list(ph_t.values()) + list(ph_wt.values()) + hr_own + hc_own
              + ph_h["t-"][0] + ph_h["t-"][1] + ph_h["t+"][0] + ph_h["t+"][1]):
        s[2]()
    for d in range(1, n_t):
        w_copy(d, it).wait_send()
        if pair:
            w_hand(d, mine).wait_send()
    for t in range(t_dev):
        for j in range(cpt):
            c = t * cpt + j
            for side, i in sides:
                for d in range(n_w - 1):
                    src = iw - d if i == 0 else iw + d
                    here = src >= 0 if i == 0 else src < n_w
                    p = piece(src, t, j * prow)

                    @pl.when(here & has[side])
                    def _():
                        rcopy(p, p, ag_s.at[i, d, c], ag_r.at[i, d, c], dev[side]).wait_send()


def local(latents, norm_gain, conv_weight, qkv_weight):
    n_t, n_h, n_w = (lax.axis_size(a) for a in ("ta", "ha", "wa"))
    t_dev, h_dev, w_dev, ch = latents.shape
    rows, cols_dev = h_dev // 2, w_dev // 2
    pd, head_dev, qkv_count, hd = qkv_weight.shape
    pc = n_w * cols_dev
    cw = conv_weight.reshape(3, 3, 3 * ch, ch)
    w2 = qkv_weight.transpose(1, 2, 0, 3).reshape(qkv_count, pd, hd)
    frames = n_t * t_dev
    chunks = t_dev * (h_dev // CH)
    vm = pl.BlockSpec(memory_space=pltpu.VMEM)
    hbm = pl.BlockSpec(memory_space=pl.ANY)
    dma = pltpu.SemaphoreType.DMA
    block_out, att = pl.pallas_call(
        functools.partial(kernel, n_t, n_h, n_w),
        out_shape=(jax.ShapeDtypeStruct(latents.shape, BF16),
                   jax.ShapeDtypeStruct((frames, rows, pc, hd), BF16)),
        in_specs=[vm, vm, hbm, hbm],
        out_specs=(vm, hbm),
        scratch_shapes=[
            pltpu.VMEM((t_dev + 2, h_dev + 2, w_dev, ch), BF16),
            pltpu.VMEM((2, t_dev, h_dev, ch), F32),
            pltpu.VMEM((2, t_dev, h_dev, ch), BF16),
            pltpu.VMEM((2, t_dev + 2, 3 * h_dev, ch), BF16),
            pltpu.VMEM((2, t_dev + 2, 3 * h_dev, ch), F32),
            pltpu.VMEM((t_dev + 2, h_dev + 2, w_dev, 3 * ch), BF16),
            pltpu.VMEM((t_dev, h_dev // CH, CH * w_dev, ch), F32),
            pltpu.VMEM((3, 3, 3 * ch, ch), BF16),
            pltpu.VMEM((n_t, qkv_count, pd, hd), BF16),
            pltpu.VMEM((ch // 128, CH * w_dev, 128), F32),
            pltpu.VMEM((n_w, t_dev, rows, cols_dev, pd), BF16),
            pltpu.VMEM((t_dev, n_t, rows, pc, hd), BF16),
            pltpu.VMEM((t_dev, rows + 2 * WIN, 2 * n_t, pc, hd), BF16),
            pltpu.VMEM((rows // WIN, WIN * pc, 3 * WIN * pc), F32),
            pltpu.VMEM((t_dev, n_t, rows, pc, hd), BF16),
            dma((2 + t_dev,)),
            dma((18,)), dma((18,)),
            dma((n_t,)), dma((n_t,)),
            dma((n_t,)), dma((n_t,)),
            dma((2, n_w, chunks)), dma((2, n_w, chunks)),
            dma((t_dev, 2)), dma((t_dev, 2)),
            dma((t_dev, n_t)), dma((t_dev, n_t)),
        ],
        compiler_params=pltpu.CompilerParams(
            collective_id=0, has_side_effects=True, vmem_limit_bytes=48 * 1024 * 1024),
    )(latents, norm_gain.reshape(1, ch), cw, w2)
    return block_out, att.reshape(frames, rows, pc, head_dev, hd)


def solution(mesh):
    return jax.shard_map(
        local,
        mesh=mesh,
        in_specs=(P("ta", "ha", "wa", None), P(), P(), P(None, ("ta", "wa"), None, None)),
        out_specs=(P("ta", "ha", "wa", None), P(None, "ha", None, ("ta", "wa"), None)),
        check_vma=False,
    )
```

time: 117 us -> 76.8 us (0.66)
  Pallas kernels: 108 us -> 71.3 us
  other arithmetic: 3.04 us -> 0 us
    pallas_call x1, Pallas kernels: 108 us -> 71.3 us  [local(): pl.pallas_call(functools.partial(kernel, n_t, n_h, n_w), out_shape=(jax.S...]
    convert_element_type x1 -> x0, other arithmetic: 1.54 us -> none  [local(): normed = jax.nn.silu(x * rms * norm_gain).astype(BF16)]
    reduce_sum x1 -> x0, other arithmetic: 1.48 us -> none  [local(): rms = lax.rsqrt(jnp.mean(x * x, axis=-1, keepdims=True) + 1e-06)]
    unnamed x5 -> x8, local copies, waits for them, and re-layouts: 3.18 us -> 4.61 us
where the time goes in v2:
time: 76.8 us; the launch traced here: 76.6 us
  Pallas kernels  71.3 us (93%)
  local copies, waits for them, and re-layouts  4.61 us (6%)
    pallas_call x1, Pallas kernels, local(): pl.pallas_call(functools.partial(kernel, n_t, n_h, n_w), out_shape=(jax.S...  71.3 us
    unnamed x8, local copies, waits for them, and re-layouts  4.61 us

profile of v2, /device:TPU:0, one launch (start us, length us, event | category | flops | bytes accessed | tf_op | source)
XLA Modules:
  0.0 76.6 jit_solution(7997751825972022594)
XLA Ops:
  0.6 0.0 copy-start
  0.6 1.1 %copy-done = bf16[1024,1,3,128]{3,0,2,1:T(8,128)(2,1)S(1)} copy-done((bf16[1024,1,3,128]{3,0,2,1:T(8,128)(2,1)S(1)}, bf16[1024,1,3,128]{3,0,2,1:T(8,128)(2,1)}, u32[]{:S(2)}) %copy-start) | copy-done | bytes 786456
  1.8 0.0 copy-start.1
  1.8 1.0 %copy-done.1 = bf16[2,16,32,256]{3,2,1,0:T(8,128)(2,1)S(1)} copy-done((bf16[2,16,32,256]{3,2,1,0:T(8,128)(2,1)S(1)}, bf16[2,16,32,256]{3,2,1,0:T(8,128)(2,1)}, u32[]{:S(2)}) %copy-start.1) | copy-done | bytes 524312
  2.8 0.0 copy-start.2
  2.8 0.7 copy-done.2
  3.5 71.3 %shard_map.59 = (bf16[2,16,32,256]{3,2,1,0:T(8,128)(2,1)S(1)}, bf16[8,8,64,128]{3,2,1,0:T(8,128)(2,1)S(1)}) custom-call(bf16[2,16,32,256]{3,2,1,0:T(8,128)(2,1)S(1)} %copy-done.1, f32[1,256]{1,0:T(1,128)S(1)} %bitcast.10, bf16[3,3,768,256]{3,2,1,0:T(8,128)(2,1)} %bitcast.11, bf16[3,1024,128]{2,1,0:T(8,128)(2,1)S(1)} %bitcast.9), custom_call_target="tpu_custom_call" | custom-call | tf_op jit(solution)/shard_map/pallas_call | solution.py:431
  74.8 0.8 %copy.9 = bf16[2,16,32,256]{3,2,1,0:T(8,128)(2,1)} copy(bf16[2,16,32,256]{3,2,1,0:T(8,128)(2,1)S(1)} %get-tuple-element.10) | data formatting | bytes 1048576
  75.6 1.0 %copy.10 = bf16[8,8,64,1,128]{4,2,3,1,0:T(8,128)(2,1)} copy(bf16[8,8,64,1,128]{4,2,3,1,0:T(8,128)(2,1)S(1)} %bitcast.8) | data formatting | bytes 2097152
Async XLA Ops:
  0.6 1.1 %copy-start = (bf16[1024,1,3,128]{3,0,2,1:T(8,128)(2,1)S(1)}, bf16[1024,1,3,128]{3,0,2,1:T(8,128)(2,1)}, u32[]{:S(2)}) copy-start(bf16[1024,1,3,128]{3,0,2,1:T(8,128)(2,1)} %param.7) | copy-start | bytes 2359300
  1.8 1.0 %copy-start.1 = (bf16[2,16,32,256]{3,2,1,0:T(8,128)(2,1)S(1)}, bf16[2,16,32,256]{3,2,1,0:T(8,128)(2,1)}, u32[]{:S(2)}) copy-start(bf16[2,16,32,256]{3,2,1,0:T(8,128)(2,1)} %latents.1) | copy-start | bytes 1572868
  2.8 0.7 copy-start.2

commit v3 on v2

--- a/solution.py
+++ b/solution.py
@@ -106,7 +106,7 @@
 
     hr_own, hc_own = rows_cols(6, own_t)
     ph_h = {"t-": rows_cols(10, pl.ds(0, 1)), "t+": rows_cols(14, pl.ds(t_dev + 1, 1))}
-    for s in list(ph_t.values()) + ph_w + hr_own:
+    for s in [ph_t["t-"]] + ph_w + hr_own:
         s[0]()
 
     def zero(cond, ref, idx, shape):
@@ -178,7 +178,8 @@
             acc_buf[t, j] = taps(acc, t, j * CH, [a for a in range(3) if 1 <= t + a <= t_dev])
 
     def halo_frame(side):
-        ph_t[side][1]()
+        if side == "t+":
+            ph_t[side][1]()
         ph_wt[side][1]()
         hs = ph_h[side][0] + ph_h[side][1]
         for s in hs:
@@ -195,8 +196,7 @@
             build(f, r)
 
     def finish(t):
-        @pl.loop(0, cpt)
-        def _(j):
+        for j in range(cpt):
             h0 = j * CH
             blk = taps(acc_buf[t, j], t, h0, [a for a in range(3) if not 1 <= t + a <= t_dev])
             blk = blk.astype(BF16)
@@ -211,14 +211,16 @@
                     for dh in range(2):
                         lo = (dh * 2 + dw) * ch + k * 128
                         pat[iw, t, pl.ds(j * prow, prow), :, lo:lo + 128] = part[:, dh]
+            if t == 0:
+                send_own(0, j)
 
     def piece(src, t, i0):
         return pat.at[src, t, pl.ds(i0, prow)]
 
     sides = (("w+", 0), ("w-", 1))
 
-    def send_own(t):
-        for j in range(cpt):
+    def send_own(t, only=None):
+        for j in range(cpt) if only is None else (only,):
             c = t * cpt + j
             p = piece(iw, t, j * prow)
             for side, i in sides:
@@ -272,78 +274,77 @@
             for d in range(1, n_t):
                 w_hand(d, theirs).wait_recv()
 
-    def qkv(t):
-        @pl.loop(0, n_t)
-        def _(a):
-            x = pat[:, t].reshape(n_w * rows * cols_dev, pd)
-            w = jnp.concatenate([wg[a, s] for s in range(3)], axis=1)
-            y = jnp.dot(x, w, preferred_element_type=F32).astype(BF16)
-            y = y.reshape(n_w, rows, cols_dev, 3 * hd)
-            for s in range(n_w):
-                cc = pl.ds(s * cols_dev, cols_dev)
-                q_buf[t, a, :, cc, :] = y[s, :, :, 0:hd]
-                kv[t, pl.ds(WIN, rows), 2 * a, cc, :] = y[s, :, :, hd:2 * hd]
-                kv[t, pl.ds(WIN, rows), 2 * a + 1, cc, :] = y[s, :, :, 2 * hd:3 * hd]
-
-    def rim(t):
-        return [halo_kv(t, 0, "h-", kv.at[t, pl.ds(WIN, WIN)], kv.at[t, pl.ds(rows + WIN, WIN)]),
-                halo_kv(t, 1, "h+", kv.at[t, pl.ds(rows, WIN)], kv.at[t, pl.ds(0, WIN)])]
-
-    def halo_kv(t, i, side, src, dst):
-        c = rcopy(src, dst, kv_s.at[t, i], kv_r.at[t, i], dev[side])
+    def head_at(step):
+        return lax.rem(it + 1 + step, n_t)
+
+    def rim(t, a):
+        lo, hi, two = pl.ds(WIN, WIN), pl.ds(rows, WIN), pl.ds(2 * a, 2)
+        return [halo_kv(t, 0, a, "h-", kv.at[t, lo, two], kv.at[t, pl.ds(rows + WIN, WIN), two]),
+                halo_kv(t, 1, a, "h+", kv.at[t, hi, two], kv.at[t, pl.ds(0, WIN), two])]
+
+    def halo_kv(t, i, a, side, src, dst):
+        c = rcopy(src, dst, kv_s.at[t, i, a], kv_r.at[t, i, a], dev[side])
         return has[side], has[side[0] + opp[side[1]]], c
 
-    def rim_start(t):
-        for out, _, c in rim(t):
+    def qkv(t, step):
+        a = head_at(step)
+        x = pat[:, t].reshape(n_w * rows * cols_dev, pd)
+        w = jnp.concatenate([wg[a, s] for s in range(3)], axis=1)
+        y = jnp.dot(x, w, preferred_element_type=F32).astype(BF16)
+        y = y.reshape(n_w, rows, cols_dev, 3 * hd)
+        for s in range(n_w):
+            cc = pl.ds(s * cols_dev, cols_dev)
+            q_buf[t, a, :, cc, :] = y[s, :, :, 0:hd]
+            kv[t, pl.ds(WIN, rows), 2 * a, cc, :] = y[s, :, :, hd:2 * hd]
+            kv[t, pl.ds(WIN, rows), 2 * a + 1, cc, :] = y[s, :, :, 2 * hd:3 * hd]
+        for out, _, c in rim(t, a):
             @pl.when(out)
             def _():
                 c.start()
 
-    def rim_recv(t):
-        for _, inn, c in rim(t):
+    scale = hd ** (-0.5) * 1.4426950408889634
+
+    def attend(t, step):
+        a = head_at(step)
+        for _, inn, c in rim(t, a):
             @pl.when(inn)
             def _():
                 c.wait_recv()
-
-    scale = hd ** (-0.5) * 1.4426950408889634
-
-    def attend(t, lo, hi):
-        @pl.loop(lo, hi)
-        def _(step):
-            a = lax.rem(it + 1 + step, n_t)
-            for b in range(rows // WIN):
-                r = pl.ds(b * WIN, WIN)
-                kr_ = pl.ds(b * WIN, 3 * WIN)
-                q = q_buf[t, a, r].reshape(WIN * pc, hd)
-                k = kv[t, kr_, 2 * a].reshape(3 * WIN * pc, hd)
-                v = kv[t, kr_, 2 * a + 1].reshape(3 * WIN * pc, hd)
-                s = lax.dot_general(q, k, (((1,), (1,)), ((), ())), preferred_element_type=F32)
-                s = s + bias[b]
-                m = jnp.max(s, axis=1, keepdims=True)
-                e = jnp.exp2((s - m) * scale)
-                z = jnp.sum(e, axis=1, keepdims=True)
-                o = jnp.dot(e.astype(BF16), v, preferred_element_type=F32) / z
-                o_buf[t, a, r] = o.astype(BF16).reshape(WIN, pc, hd)
-            dst = out_att.at[it * t_dev + t]
-
-            @pl.when(a != it)
-            def _():
-                rcopy(o_buf.at[t, a], dst, at_s.at[t, a], at_r.at[t, it], {"ta": a}).start()
-
-            @pl.when(a == it)
-            def _():
-                pltpu.make_async_copy(o_buf.at[t, a], dst, loc_sem.at[2 + t]).start()
+        for b in range(rows // WIN):
+            r = pl.ds(b * WIN, WIN)
+            kr_ = pl.ds(b * WIN, 3 * WIN)
+            q = q_buf[t, a, r].reshape(WIN * pc, hd)
+            k = kv[t, kr_, 2 * a].reshape(3 * WIN * pc, hd)
+            v = kv[t, kr_, 2 * a + 1].reshape(3 * WIN * pc, hd)
+            s = lax.dot_general(q, k, (((1,), (1,)), ((), ())), preferred_element_type=F32)
+            s = s + bias[b]
+            m = jnp.max(s, axis=1, keepdims=True)
+            e = jnp.exp2((s - m) * scale)
+            z = jnp.sum(e, axis=1, keepdims=True)
+            o = jnp.dot(e.astype(BF16), v, preferred_element_type=F32) / z
+            o_buf[t, a, r] = o.astype(BF16).reshape(WIN, pc, hd)
+        dst = out_att.at[it * t_dev + t]
+
+        @pl.when(a != it)
+        def _():
+            rcopy(o_buf.at[t, a], dst, at_s.at[t, a], at_r.at[t, it], {"ta": a}).start()
+
+        @pl.when(a == it)
+        def _():
+            pltpu.make_async_copy(o_buf.at[t, a], dst, loc_sem.at[2 + t]).start()
+
+    ph_t["t-"][1]()
+    ph_t["t+"][0]()
+    w_start()
 
     halo_frame("t-")
     if t_dev == 1:
         halo_frame("t+")
     finish(0)
-    send_own(0)
     for t in range(1, t_dev):
         if t == t_dev - 1:
             halo_frame("t+")
         finish(t)
-    w_start()
 
     total_rows = rows * n_h
     bs = (WIN * pc, 3 * WIN * pc)
@@ -364,20 +365,26 @@
     w_end()
     for t in range(t_dev):
         more = t + 1 < t_dev
-        qkv(t)
-        rim_start(t)
-        steps = n_w - 2
-        rim_done = False
-        for d in range(1, n_w - 1):
-            if more:
-                relay(t + 1, d)
-            if not rim_done:
-                rim_recv(t)
-                rim_done = True
-            attend(t, n_t * (d - 1) // steps, n_t * d // steps)
-        if not rim_done:
-            rim_recv(t)
-            attend(t, 0, n_t)
+        if more:
+            @pl.loop(0, n_t)
+            def _(step):
+                qkv(t, step)
+            steps = max(n_w - 2, 1)
+            for d in range(1, steps + 1):
+                if d < n_w - 1:
+                    relay(t + 1, d)
+
+                @pl.loop(n_t * (d - 1) // steps, n_t * d // steps)
+                def _(step):
+                    attend(t, step)
+        else:
+            qkv(t, 0)
+
+            @pl.loop(0, n_t - 1)
+            def _(step):
+                qkv(t, step + 1)
+                attend(t, step)
+            attend(t, n_t - 1)
         if more:
             if t + 2 < t_dev:
                 send_own(t + 2)
@@ -390,10 +397,11 @@
             src = lax.rem(it + d, n_t)
             rcopy(o_buf.at[t, src], out_att.at[src * t_dev + t], at_s.at[t, src], at_r.at[t, src],
                   {"ta": src}).wait()
-        for out, _, c in rim(t):
-            @pl.when(out)
-            def _():
-                c.wait_send()
+        for a in range(n_t):
+            for out, _, c in rim(t, a):
+                @pl.when(out)
+                def _():
+                    c.wait_send()
     for s in (ph_w + list(ph_t.values()) + list(ph_wt.values()) + hr_own + hc_own
               + ph_h["t-"][0] + ph_h["t-"][1] + ph_h["t+"][0] + ph_h["t+"][1]):
         s[2]()
@@ -455,11 +463,11 @@
             dma((n_t,)), dma((n_t,)),
             dma((n_t,)), dma((n_t,)),
             dma((2, n_w, chunks)), dma((2, n_w, chunks)),
-            dma((t_dev, 2)), dma((t_dev, 2)),
+            dma((t_dev, 2, n_t)), dma((t_dev, 2, n_t)),
             dma((t_dev, n_t)), dma((t_dev, n_t)),
         ],
         compiler_params=pltpu.CompilerParams(
-            collective_id=0, has_side_effects=True, vmem_limit_bytes=48 * 1024 * 1024),
+            collective_id=0, has_side_effects=True, vmem_limit_bytes=60 * 1024 * 1024),
     )(latents, norm_gain.reshape(1, ch), cw, w2)
     return block_out, att.reshape(frames, rows, pc, head_dev, hd)
 

time: 76.8 us -> 73.3 us (0.954)
  Pallas kernels: 71.3 us -> 68.3 us
    pallas_call x1, Pallas kernels: 71.3 us -> 68.3 us  [local(): pl.pallas_call(functools.partial(kernel, n_t, n_h, n_w), out_shape=(jax.S...]
    unnamed x8 -> x2, local copies, waits for them, and re-layouts: 4.61 us -> 4.13 us
where the time goes in v3:
time: 73.3 us; the launch traced here: 73 us
  Pallas kernels  68.3 us (93%)
  local copies, waits for them, and re-layouts  4.13 us (6%)
    pallas_call x1, Pallas kernels, local(): pl.pallas_call(functools.partial(kernel, n_t, n_h, n_w), out_shape=(jax.S...  68.3 us
    unnamed x2, local copies, waits for them, and re-layouts  4.13 us

profile of v3, /device:TPU:0, one launch (start us, length us, event | category | flops | bytes accessed | tf_op | source)
XLA Modules:
  0.0 73.0 jit_solution(4501578359046193361)
XLA Ops:
  0.6 68.3 %shard_map.59 = (bf16[2,16,32,256]{3,2,1,0:T(8,128)(2,1)}, bf16[8,8,64,128]{3,2,1,0:T(8,128)(2,1)}) custom-call(bf16[2,16,32,256]{3,2,1,0:T(8,128)(2,1)} %latents.1, f32[1,256]{1,0:T(1,128)} %bitcast.11, bf16[3,3,768,256]{3,2,1,0:T(8,128)(2,1)} %bitcast.8, bf16[3,1024,128]{2,1,0:T(8,128)(2,1)} %bitcast.10), custom_call_target="tpu_custom_call" | custom-call | tf_op jit(solution)/shard_map/pallas_call | solution.py:439
  68.9 1.9 %copy.9 = bf16[2,16,32,256]{3,2,1,0:T(8,128)(2,1)} copy(bf16[2,16,32,256]{3,2,1,0:T(8,128)(2,1)} %get-tuple-element.10) | data formatting | bytes 1048576
  70.8 2.3 %copy.10 = bf16[8,8,64,1,128]{4,2,3,1,0:T(8,128)(2,1)} copy(bf16[8,8,64,1,128]{4,2,3,1,0:T(8,128)(2,1)} %bitcast.9) | data formatting | bytes 2097152

commit v4 on v3

--- a/solution.py
+++ b/solution.py
@@ -14,8 +14,8 @@
 BF16 = jnp.bfloat16
 
 
-def kernel(n_t, n_h, n_w, latents, gain, cw_hbm, w_hbm, out_block, out_att,
-           pad_n, edge_f, edge_b, pad_c, cf, x3, acc_buf, cw, wg, fbuf, pat, q_buf, kv, bias, o_buf,
+def kernel(n_t, n_h, n_w, lat_hbm, gain_hbm, cw_hbm, w_hbm, blk_hbm, out_att,
+           out_block, latents, gain, raw, pad_n, edge_f, edge_b, pad_c, cf, x3, acc_buf, cw, wg, fbuf, pat, q_buf, kv, bias, o_buf,
            loc_sem, halo_s, halo_r, w_s, w_r, wf_s, wf_r, ag_s, ag_r, kv_s, kv_r, at_s, at_r):
     t_dev, h_dev, w_dev, ch = latents.shape
     rows = h_dev // 2
@@ -36,6 +36,10 @@
         return pltpu.make_async_remote_copy(
             src_ref=src, dst_ref=dst, send_sem=ss, recv_sem=rs, device_id=device, device_id_type=MESH)
 
+    lat_copy = pltpu.make_async_copy(lat_hbm, latents, loc_sem.at[2 + t_dev])
+    lat_copy.start()
+    gain_copy = pltpu.make_async_copy(gain_hbm, gain, loc_sem.at[3 + t_dev])
+    gain_copy.start()
     cw_copy = pltpu.make_async_copy(cw_hbm, cw, loc_sem.at[0])
     cw_copy.start()
     own_w = pltpu.make_async_copy(w_hbm, wg.at[it], loc_sem.at[1])
@@ -52,18 +56,6 @@
     for d in range(1, n_t):
         pl.semaphore_signal(bar, inc=1, device_id={"ta": lax.rem(it + d, n_t)}, device_id_type=MESH)
 
-    @pl.loop(0, t_dev)
-    def _(t):
-        for r in range(h_dev):
-            x = latents[t, r].astype(F32)
-            ms = jnp.sum(x * x, axis=-1, keepdims=True) * (1.0 / ch)
-            n = x * lax.rsqrt(ms + 1e-06) * gain[...]
-            n = n / (1.0 + jnp.exp(-n))
-            pad_n[t + 1, r + 1] = n.astype(BF16)
-            edge_f[0, t, r:r + 1, :] = n[0:1]
-            edge_f[1, t, r:r + 1, :] = n[w_dev - 1:w_dev]
-
-    edge_b[...] = edge_f[...].astype(BF16)
     pl.semaphore_wait(bar, count)
 
     def halo(i, side, src, dst):
@@ -93,8 +85,8 @@
     own_h = pl.ds(1, h_dev)
     ph_w = [halo(0, "w-", edge_b.at[0], pad_c.at[1, own_t, own]),
             halo(1, "w+", edge_b.at[1], pad_c.at[0, own_t, own])]
-    ph_t = {"t+": halo(2, "t-", pad_n.at[1, own_h], pad_n.at[t_dev + 1, own_h]),
-            "t-": halo(3, "t+", pad_n.at[t_dev, own_h], pad_n.at[0, own_h])}
+    ph_t = {"t+": halo(2, "t-", lat_hbm.at[0], raw.at[1]),
+            "t-": halo(3, "t+", lat_hbm.at[t_dev - 1], raw.at[0])}
     ph_wt = {"t+": halo(4, "t-", pad_c.at[:, 1, own], pad_c.at[:, t_dev + 1, own]),
              "t-": halo(5, "t+", pad_c.at[:, t_dev, own], pad_c.at[:, 0, own])}
 
@@ -106,7 +98,28 @@
 
     hr_own, hc_own = rows_cols(6, own_t)
     ph_h = {"t-": rows_cols(10, pl.ds(0, 1)), "t+": rows_cols(14, pl.ds(t_dev + 1, 1))}
-    for s in [ph_t["t-"]] + ph_w + hr_own:
+    ph_t["t-"][0]()
+
+    def norm(x16):
+        x = x16.astype(F32)
+        ms = jnp.sum(x * x, axis=-1, keepdims=True) * (1.0 / ch)
+        n = x * lax.rsqrt(ms + 1e-06) * half_gain
+        return n * jnp.tanh(n) + n
+
+    lat_copy.wait()
+    gain_copy.wait()
+    half_gain = gain[...] * 0.5
+
+    @pl.loop(0, t_dev)
+    def _(t):
+        for r in range(h_dev):
+            n = norm(latents[t, r])
+            pad_n[t + 1, r + 1] = n.astype(BF16)
+            edge_f[0, t, r:r + 1, :] = n[0:1]
+            edge_f[1, t, r:r + 1, :] = n[w_dev - 1:w_dev]
+
+    edge_b[...] = edge_f[...].astype(BF16)
+    for s in ph_w + hr_own:
         s[0]()
 
     def zero(cond, ref, idx, shape):
@@ -120,7 +133,7 @@
         zero(no[side], pad_c, (s, own_t, own), (t_dev, h_dev, ch))
     for side, t in (("t-", 0), ("t+", t_dev + 1)):
         zero(no[side], pad_c, (full, t, own), (2, h_dev, ch))
-        zero(no[side], pad_n, (t, own_h), (h_dev, w_dev, ch))
+        zero(no[side], raw, (0 if t == 0 else 1,), (h_dev, w_dev, ch))
     for side, r, b in (("h-", 0, low), ("h+", h_dev + 1, high)):
         zero(no[side], pad_n, (full, r), (t_dev + 2, w_dev, ch))
         zero(no[side], pad_c, (full, full, b), (2, t_dev + 2, h_dev, ch))
@@ -151,17 +164,18 @@
         for r in range(1, h_dev + 1):
             build(t, r)
 
-    for s in hr_own + hc_own:
-        s[1]()
-    for b in (low, high):
-        cf[:, own_t, b] = pad_c[:, own_t, b].astype(F32)
-
-    @pl.loop(1, t_dev + 1)
-    def _(t):
-        for r in (0, h_dev + 1):
-            build(t, r)
-
-    cw_copy.wait()
+    def early_edges():
+        for s in hr_own + hc_own:
+            s[1]()
+        for b in (low, high):
+            cf[:, own_t, b] = pad_c[:, own_t, b].astype(F32)
+
+        @pl.loop(1, t_dev + 1)
+        def _(t):
+            for r in (0, h_dev + 1):
+                build(t, r)
+
+        cw_copy.wait()
 
     def taps(acc, t, h0, frames):
         for a in frames:
@@ -171,29 +185,38 @@
                     preferred_element_type=F32)
         return acc
 
-    for t in range(t_dev):
+    def start_taps(t):
         @pl.loop(0, cpt)
         def _(j):
             acc = latents[t, pl.ds(j * CH, CH)].astype(F32).reshape(CH * w_dev, ch)
             acc_buf[t, j] = taps(acc, t, j * CH, [a for a in range(3) if 1 <= t + a <= t_dev])
 
-    def halo_frame(side):
-        if side == "t+":
-            ph_t[side][1]()
+    frame_of = {"t-": 0, "t+": t_dev + 1}
+
+    def halo_in(side):
+        f = frame_of[side]
+        for r in range(h_dev):
+            pad_n[f, r + 1] = norm(raw[0 if f == 0 else 1, r]).astype(BF16)
+        for s in ph_h[side][0]:
+            s[0]()
         ph_wt[side][1]()
-        hs = ph_h[side][0] + ph_h[side][1]
-        for s in hs:
+        for s in ph_h[side][1]:
             s[0]()
-        f = 0 if side == "t-" else t_dev + 1
         cf[:, f, own] = pad_c[:, f, own].astype(F32)
         for r in range(1, h_dev + 1):
             build(f, r)
-        for s in hs:
+
+    def halo_end(side):
+        f = frame_of[side]
+        for s in ph_h[side][0] + ph_h[side][1]:
             s[1]()
         for b in (low, high):
             cf[:, f, b] = pad_c[:, f, b].astype(F32)
         for r in (0, h_dev + 1):
             build(f, r)
+
+    def blk_copy(t):
+        return pltpu.make_async_copy(out_block.at[t], blk_hbm.at[t], loc_sem.at[4 + t_dev + t])
 
     def finish(t):
         for j in range(cpt):
@@ -213,6 +236,7 @@
                         pat[iw, t, pl.ds(j * prow, prow), :, lo:lo + 128] = part[:, dh]
             if t == 0:
                 send_own(0, j)
+        blk_copy(t).start()
 
     def piece(src, t, i0):
         return pat.at[src, t, pl.ds(i0, prow)]
@@ -337,13 +361,23 @@
     ph_t["t+"][0]()
     w_start()
 
-    halo_frame("t-")
+    halo_in("t-")
     if t_dev == 1:
-        halo_frame("t+")
+        ph_t["t+"][1]()
+        halo_in("t+")
+    early_edges()
+    start_taps(0)
+    halo_end("t-")
+    if t_dev == 1:
+        halo_end("t+")
     finish(0)
     for t in range(1, t_dev):
         if t == t_dev - 1:
-            halo_frame("t+")
+            ph_t["t+"][1]()
+            halo_in("t+")
+        start_taps(t)
+        if t == t_dev - 1:
+            halo_end("t+")
         finish(t)
 
     total_rows = rows * n_h
@@ -392,6 +426,7 @@
                 relay(t + 1, n_w - 1)
 
     for t in range(t_dev):
+        blk_copy(t).wait()
         pltpu.make_async_copy(o_buf.at[t, it], out_att.at[it * t_dev + t], loc_sem.at[2 + t]).wait()
         for d in range(1, n_t):
             src = lax.rem(it + d, n_t)
@@ -423,6 +458,17 @@
                         rcopy(p, p, ag_s.at[i, d, c], ag_r.at[i, d, c], dev[side]).wait_send()
 
 
+def results(block, att, out_block, out_att, sem):
+    copies = [pltpu.make_async_copy(block.at[i], out_block.at[i], sem.at[i])
+              for i in range(block.shape[0])]
+    copies += [pltpu.make_async_copy(att.at[i], out_att.at[i], sem.at[block.shape[0] + i])
+               for i in range(att.shape[0])]
+    for c in copies:
+        c.start()
+    for c in copies:
+        c.wait()
+
+
 def local(latents, norm_gain, conv_weight, qkv_weight):
     n_t, n_h, n_w = (lax.axis_size(a) for a in ("ta", "ha", "wa"))
     t_dev, h_dev, w_dev, ch = latents.shape
@@ -433,16 +479,19 @@
     w2 = qkv_weight.transpose(1, 2, 0, 3).reshape(qkv_count, pd, hd)
     frames = n_t * t_dev
     chunks = t_dev * (h_dev // CH)
-    vm = pl.BlockSpec(memory_space=pltpu.VMEM)
-    hbm = pl.BlockSpec(memory_space=pl.ANY)
+    hbm = pl.BlockSpec(memory_space=pltpu.HBM)
     dma = pltpu.SemaphoreType.DMA
     block_out, att = pl.pallas_call(
         functools.partial(kernel, n_t, n_h, n_w),
         out_shape=(jax.ShapeDtypeStruct(latents.shape, BF16),
                    jax.ShapeDtypeStruct((frames, rows, pc, hd), BF16)),
-        in_specs=[vm, vm, hbm, hbm],
-        out_specs=(vm, hbm),
+        in_specs=[hbm, hbm, hbm, hbm],
+        out_specs=(hbm, hbm),
         scratch_shapes=[
+            pltpu.VMEM(latents.shape, BF16),
+            pltpu.VMEM(latents.shape, BF16),
+            pltpu.VMEM((1, ch), F32),
+            pltpu.VMEM((2, h_dev, w_dev, ch), BF16),
             pltpu.VMEM((t_dev + 2, h_dev + 2, w_dev, ch), BF16),
             pltpu.VMEM((2, t_dev, h_dev, ch), F32),
             pltpu.VMEM((2, t_dev, h_dev, ch), BF16),
@@ -458,7 +507,7 @@
             pltpu.VMEM((t_dev, rows + 2 * WIN, 2 * n_t, pc, hd), BF16),
             pltpu.VMEM((rows // WIN, WIN * pc, 3 * WIN * pc), F32),
             pltpu.VMEM((t_dev, n_t, rows, pc, hd), BF16),
-            dma((2 + t_dev,)),
+            dma((4 + 2 * t_dev,)),
             dma((18,)), dma((18,)),
             dma((n_t,)), dma((n_t,)),
             dma((n_t,)), dma((n_t,)),
@@ -467,8 +516,15 @@
             dma((t_dev, n_t)), dma((t_dev, n_t)),
         ],
         compiler_params=pltpu.CompilerParams(
-            collective_id=0, has_side_effects=True, vmem_limit_bytes=60 * 1024 * 1024),
+            collective_id=0, has_side_effects=True, vmem_limit_bytes=58 * 1024 * 1024),
     )(latents, norm_gain.reshape(1, ch), cw, w2)
+    block_out, att = pl.pallas_call(
+        results,
+        out_shape=(jax.ShapeDtypeStruct(block_out.shape, BF16), jax.ShapeDtypeStruct(att.shape, BF16)),
+        in_specs=[hbm, hbm],
+        out_specs=(hbm, hbm),
+        scratch_shapes=[dma((t_dev + frames,))],
+    )(block_out, att)
     return block_out, att.reshape(frames, rows, pc, head_dev, hd)
 
 

time: 73.3 us -> 116 us (1.58)
  Pallas kernels: 68.3 us -> 116 us
  local copies, waits for them, and re-layouts: 4.13 us -> 0 us
    pallas_call x0 -> x1, Pallas kernels: none -> 48.8 us  [local(): pl.pallas_call(results, out_shape=(jax.ShapeDtypeStruct(block_out.shape,...]
    unnamed x2 -> x0, local copies, waits for them, and re-layouts: 4.13 us -> none
    pallas_call x1, Pallas kernels: 68.3 us -> 66.7 us  [local(): pl.pallas_call(functools.partial(kernel, n_t, n_h, n_w), out_shape=(jax.S...]
where the time goes in v4:
time: 116 us
  Pallas kernels  116 us (100%)
    pallas_call x1, Pallas kernels, local(): pl.pallas_call(functools.partial(kernel, n_t, n_h, n_w), out_shape=(jax.S...  66.7 us
    pallas_call x1, Pallas kernels, local(): pl.pallas_call(results, out_shape=(jax.ShapeDtypeStruct(block_out.shape,...  48.8 us

profile of v4, /device:TPU:0, one launch (start us, length us, event | category | flops | bytes accessed | tf_op | source)
XLA Modules:
  0.0 116.2 jit_solution(432665671615039866)
XLA Ops:
  0.6 66.7 %shard_map.59 = (bf16[2,16,32,256]{3,2,1,0:T(8,128)(2,1)}, bf16[8,8,64,128]{3,2,1,0:T(8,128)(2,1)}) custom-call(bf16[2,16,32,256]{3,2,1,0:T(8,128)(2,1)} %lat_hbm.1, f32[1,256]{1,0:T(1,128)} %bitcast.10, bf16[3,3,768,256]{3,2,1,0:T(8,128)(2,1)} %bitcast.8, bf16[3,1024,128]{2,1,0:T(8,128)(2,1)} %bitcast.9), custom_call_target="tpu_custom_call" | custom-call | tf_op jit(solution)/shard_map/pallas_call | solution.py:484
  67.3 48.8 %shard_map.60 = (bf16[2,16,32,256]{3,2,1,0:T(8,128)(2,1)}, bf16[8,8,64,128]{3,2,1,0:T(8,128)(2,1)}) custom-call(bf16[2,16,32,256]{3,2,1,0:T(8,128)(2,1)} %get-tuple-element.6.block, bf16[8,8,64,128]{3,2,1,0:T(8,128)(2,1)} %get-tuple-element.7.att), custom_call_target="tpu_custom_call" | custom-call | tf_op jit(solution)/shard_map/pallas_call | solution.py:521

commit v5 on v4

--- a/solution.py
+++ b/solution.py
@@ -8,6 +8,7 @@
 from jax.sharding import PartitionSpec as P
 
 WIN = 4
+STRIP = 32
 CH = 8
 MESH = pl.DeviceIdType.MESH
 F32 = jnp.float32
@@ -15,7 +16,7 @@
 
 
 def kernel(n_t, n_h, n_w, lat_hbm, gain_hbm, cw_hbm, w_hbm, blk_hbm, out_att,
-           out_block, latents, gain, raw, pad_n, edge_f, edge_b, pad_c, cf, x3, acc_buf, cw, wg, fbuf, pat, q_buf, kv, bias, o_buf,
+           out_block, latents, gain, raw, pad_n, edge_f, edge_b, pad_c, cf, x3, acc_buf, cw, wg, fbuf, pat, q_buf, kv, bias, s_buf, p_buf, o_buf,
            loc_sem, halo_s, halo_r, w_s, w_r, wf_s, wf_r, ag_s, ag_r, kv_s, kv_r, at_s, at_r):
     t_dev, h_dev, w_dev, ch = latents.shape
     rows = h_dev // 2
@@ -328,6 +329,11 @@
 
     scale = hd ** (-0.5) * 1.4426950408889634
 
+    def window(i):
+        lo = i // pc * pc // 128 * 128
+        hi = min(-(-(((i + STRIP - 1) // pc + 2 * WIN + 1) * pc) // 128) * 128, 3 * WIN * pc)
+        return pl.ds(lo, hi - lo)
+
     def attend(t, step):
         a = head_at(step)
         for _, inn, c in rim(t, a):
@@ -340,12 +346,17 @@
             q = q_buf[t, a, r].reshape(WIN * pc, hd)
             k = kv[t, kr_, 2 * a].reshape(3 * WIN * pc, hd)
             v = kv[t, kr_, 2 * a + 1].reshape(3 * WIN * pc, hd)
-            s = lax.dot_general(q, k, (((1,), (1,)), ((), ())), preferred_element_type=F32)
-            s = s + bias[b]
-            m = jnp.max(s, axis=1, keepdims=True)
-            e = jnp.exp2((s - m) * scale)
-            z = jnp.sum(e, axis=1, keepdims=True)
-            o = jnp.dot(e.astype(BF16), v, preferred_element_type=F32) / z
+            s_buf[b] = lax.dot_general(q, k, (((1,), (1,)), ((), ())), preferred_element_type=F32)
+            inv = []
+            for i in range(0, WIN * pc, STRIP):
+                at = (b, pl.ds(i, STRIP), window(i))
+                s = s_buf[at] + bias[at]
+                m = jnp.max(s, axis=1, keepdims=True)
+                e = jnp.exp2((s - m) * scale)
+                inv.append(1.0 / jnp.sum(e, axis=1, keepdims=True))
+                p_buf[at] = e.astype(BF16)
+            o = jnp.dot(p_buf[b], v, preferred_element_type=F32)
+            o = o * jnp.concatenate(inv, axis=0)
             o_buf[t, a, r] = o.astype(BF16).reshape(WIN, pc, hd)
         dst = out_att.at[it * t_dev + t]
 
@@ -388,6 +399,7 @@
         kg = ih * rows + b * WIN + kr
         ok = (jnp.abs(qr - kr) <= WIN) & (kg >= 0) & (kg < total_rows)
         bias[b] = jnp.where(ok, 0.0, -1e30).astype(F32)
+        p_buf[b] = jnp.zeros(bs, BF16)
 
     for d in range(1, n_w - 1):
         relay(0, d)
@@ -459,10 +471,8 @@
 
 
 def results(block, att, out_block, out_att, sem):
-    copies = [pltpu.make_async_copy(block.at[i], out_block.at[i], sem.at[i])
-              for i in range(block.shape[0])]
-    copies += [pltpu.make_async_copy(att.at[i], out_att.at[i], sem.at[block.shape[0] + i])
-               for i in range(att.shape[0])]
+    copies = [pltpu.make_async_copy(block, out_block, sem.at[0]),
+              pltpu.make_async_copy(att, out_att, sem.at[1])]
     for c in copies:
         c.start()
     for c in copies:
@@ -479,6 +489,7 @@
     w2 = qkv_weight.transpose(1, 2, 0, 3).reshape(qkv_count, pd, hd)
     frames = n_t * t_dev
     chunks = t_dev * (h_dev // CH)
+    vm = pl.BlockSpec(memory_space=pltpu.VMEM)
     hbm = pl.BlockSpec(memory_space=pltpu.HBM)
     dma = pltpu.SemaphoreType.DMA
     block_out, att = pl.pallas_call(
@@ -506,6 +517,8 @@
             pltpu.VMEM((t_dev, n_t, rows, pc, hd), BF16),
             pltpu.VMEM((t_dev, rows + 2 * WIN, 2 * n_t, pc, hd), BF16),
             pltpu.VMEM((rows // WIN, WIN * pc, 3 * WIN * pc), F32),
+            pltpu.VMEM((rows // WIN, WIN * pc, 3 * WIN * pc), F32),
+            pltpu.VMEM((rows // WIN, WIN * pc, 3 * WIN * pc), BF16),
             pltpu.VMEM((t_dev, n_t, rows, pc, hd), BF16),
             dma((4 + 2 * t_dev,)),
             dma((18,)), dma((18,)),
@@ -521,9 +534,9 @@
     block_out, att = pl.pallas_call(
         results,
         out_shape=(jax.ShapeDtypeStruct(block_out.shape, BF16), jax.ShapeDtypeStruct(att.shape, BF16)),
-        in_specs=[hbm, hbm],
+        in_specs=[vm, vm],
         out_specs=(hbm, hbm),
-        scratch_shapes=[dma((t_dev + frames,))],
+        scratch_shapes=[dma((2,))],
     )(block_out, att)
     return block_out, att.reshape(frames, rows, pc, head_dev, hd)
 

time: 116 us -> 70.1 us (0.60)
  Pallas kernels: 116 us -> 69.3 us
    pallas_call x1, Pallas kernels: 48.8 us -> 2.55 us  [local(): pl.pallas_call(results, out_shape=(jax.ShapeDtypeStruct(block_out.shape,...]
where the time goes in v5:
time: 70.1 us; the launch traced here: 70 us
  Pallas kernels  69.3 us (99%)
    pallas_call x1, Pallas kernels, local(): pl.pallas_call(functools.partial(kernel, n_t, n_h, n_w), out_shape=(jax.S...  66.8 us
    pallas_call x1, Pallas kernels, local(): pl.pallas_call(results, out_shape=(jax.ShapeDtypeStruct(block_out.shape,...  2.55 us

profile of v5, /device:TPU:0, one launch (start us, length us, event | category | flops | bytes accessed | tf_op | source)
XLA Modules:
  0.0 70.0 jit_solution(6778880486373454751)
XLA Ops:
  0.6 66.8 %shard_map.59 = (bf16[2,16,32,256]{3,2,1,0:T(8,128)(2,1)}, bf16[8,8,64,128]{3,2,1,0:T(8,128)(2,1)}) custom-call(bf16[2,16,32,256]{3,2,1,0:T(8,128)(2,1)} %lat_hbm.1, f32[1,256]{1,0:T(1,128)} %bitcast.10, bf16[3,3,768,256]{3,2,1,0:T(8,128)(2,1)} %bitcast.8, bf16[3,1024,128]{2,1,0:T(8,128)(2,1)} %bitcast.9), custom_call_target="tpu_custom_call" | custom-call | tf_op jit(solution)/shard_map/pallas_call | solution.py:495
  67.4 2.5 %shard_map.60 = (bf16[2,16,32,256]{3,2,1,0:T(8,128)(2,1)}, bf16[8,8,64,128]{3,2,1,0:T(8,128)(2,1)}) custom-call(bf16[2,16,32,256]{3,2,1,0:T(8,128)(2,1)} %get-tuple-element.6.block, bf16[8,8,64,128]{3,2,1,0:T(8,128)(2,1)} %get-tuple-element.7.att), custom_call_target="tpu_custom_call" | custom-call | tf_op jit(solution)/shard_map/pallas_call | solution.py:534

commit v6 on v5

--- a/solution.py
+++ b/solution.py
@@ -235,8 +235,7 @@
                     for dh in range(2):
                         lo = (dh * 2 + dw) * ch + k * 128
                         pat[iw, t, pl.ds(j * prow, prow), :, lo:lo + 128] = part[:, dh]
-            if t == 0:
-                send_own(0, j)
+            send_own(t, j)
         blk_copy(t).start()
 
     def piece(src, t, i0):
@@ -283,9 +282,12 @@
         src = lax.rem(it + n_t - d, n_t)
         return rcopy(wg.at[src, :, part], wg.at[src, :, part], wf_s.at[d], wf_r.at[d], other)
 
-    def w_start():
-        for d in range(1, n_t):
+    w_left = list(range(1, n_t))
+
+    def w_next(count=1):
+        for d in w_left[:count]:
             w_copy(d, it).start()
+        del w_left[:count]
 
     def w_mid():
         for d in range(1, n_t):
@@ -370,7 +372,6 @@
 
     ph_t["t-"][1]()
     ph_t["t+"][0]()
-    w_start()
 
     halo_in("t-")
     if t_dev == 1:
@@ -382,6 +383,7 @@
     if t_dev == 1:
         halo_end("t+")
     finish(0)
+    w_next()
     for t in range(1, t_dev):
         if t == t_dev - 1:
             ph_t["t+"][1]()
@@ -390,6 +392,7 @@
         if t == t_dev - 1:
             halo_end("t+")
         finish(t)
+        w_next()
 
     total_rows = rows * n_h
     bs = (WIN * pc, 3 * WIN * pc)
@@ -402,27 +405,25 @@
         p_buf[b] = jnp.zeros(bs, BF16)
 
     for d in range(1, n_w - 1):
-        relay(0, d)
-    if t_dev > 1:
-        send_own(1)
+        for t in range(t_dev):
+            relay(t, d)
+        w_next()
+    w_next(n_t)
     w_mid()
     if n_w > 1:
         relay(0, n_w - 1)
     w_end()
     for t in range(t_dev):
-        more = t + 1 < t_dev
-        if more:
+        if t + 1 < t_dev:
             @pl.loop(0, n_t)
             def _(step):
                 qkv(t, step)
-            steps = max(n_w - 2, 1)
-            for d in range(1, steps + 1):
-                if d < n_w - 1:
-                    relay(t + 1, d)
-
-                @pl.loop(n_t * (d - 1) // steps, n_t * d // steps)
-                def _(step):
-                    attend(t, step)
+
+            @pl.loop(0, n_t)
+            def _(step):
+                attend(t, step)
+            if n_w > 1:
+                relay(t + 1, n_w - 1)
         else:
             qkv(t, 0)
 
@@ -431,11 +432,6 @@
                 qkv(t, step + 1)
                 attend(t, step)
             attend(t, n_t - 1)
-        if more:
-            if t + 2 < t_dev:
-                send_own(t + 2)
-            if n_w > 1:
-                relay(t + 1, n_w - 1)
 
     for t in range(t_dev):
         blk_copy(t).wait()

time: 70.1 us -> 71.4 us (1.019)
  Pallas kernels: 69.3 us -> 70.6 us
    pallas_call x1, Pallas kernels: 66.8 us -> 68.1 us  [local(): pl.pallas_call(functools.partial(kernel, n_t, n_h, n_w), out_shape=(jax.S...]
where the time goes in v6:
time: 71.4 us; the launch traced here: 71.3 us
  Pallas kernels  70.6 us (99%)
    pallas_call x1, Pallas kernels, local(): pl.pallas_call(functools.partial(kernel, n_t, n_h, n_w), out_shape=(jax.S...  68.1 us
    pallas_call x1, Pallas kernels, local(): pl.pallas_call(results, out_shape=(jax.ShapeDtypeStruct(block_out.shape,...  2.55 us

profile of v6, /device:TPU:0, one launch (start us, length us, event | category | flops | bytes accessed | tf_op | source)
XLA Modules:
  0.0 71.3 jit_solution(13219771422265723595)
XLA Ops:
  0.6 68.1 %shard_map.59 = (bf16[2,16,32,256]{3,2,1,0:T(8,128)(2,1)}, bf16[8,8,64,128]{3,2,1,0:T(8,128)(2,1)}) custom-call(bf16[2,16,32,256]{3,2,1,0:T(8,128)(2,1)} %lat_hbm.1, f32[1,256]{1,0:T(1,128)} %bitcast.10, bf16[3,3,768,256]{3,2,1,0:T(8,128)(2,1)} %bitcast.8, bf16[3,1024,128]{2,1,0:T(8,128)(2,1)} %bitcast.9), custom_call_target="tpu_custom_call" | custom-call | tf_op jit(solution)/shard_map/pallas_call | solution.py:491
  68.7 2.5 %shard_map.60 = (bf16[2,16,32,256]{3,2,1,0:T(8,128)(2,1)}, bf16[8,8,64,128]{3,2,1,0:T(8,128)(2,1)}) custom-call(bf16[2,16,32,256]{3,2,1,0:T(8,128)(2,1)} %get-tuple-element.6.block, bf16[8,8,64,128]{3,2,1,0:T(8,128)(2,1)} %get-tuple-element.7.att), custom_call_target="tpu_custom_call" | custom-call | tf_op jit(solution)/shard_map/pallas_call | solution.py:530

commit v7 on v5

--- a/solution.py
+++ b/solution.py
@@ -9,7 +9,8 @@
 
 WIN = 4
 STRIP = 32
-CH = 8
+CH = 16
+PH = 8
 MESH = pl.DeviceIdType.MESH
 F32 = jnp.float32
 BF16 = jnp.bfloat16
@@ -26,6 +27,8 @@
     pc = n_w * cols_dev
     cpt = h_dev // CH
     prow = CH // 2
+    ppt = h_dev // PH
+    srow = PH // 2
     it, ih, iw = lax.axis_index("ta"), lax.axis_index("ha"), lax.axis_index("wa")
     has = {"t-": it > 0, "t+": it < n_t - 1, "h-": ih > 0, "h+": ih < n_h - 1,
            "w-": iw > 0, "w+": iw < n_w - 1}
@@ -236,30 +239,31 @@
                         lo = (dh * 2 + dw) * ch + k * 128
                         pat[iw, t, pl.ds(j * prow, prow), :, lo:lo + 128] = part[:, dh]
             if t == 0:
-                send_own(0, j)
+                for i in range(CH // PH):
+                    send_own(0, j * (CH // PH) + i)
         blk_copy(t).start()
 
     def piece(src, t, i0):
-        return pat.at[src, t, pl.ds(i0, prow)]
+        return pat.at[src, t, pl.ds(i0, srow)]
 
     sides = (("w+", 0), ("w-", 1))
 
     def send_own(t, only=None):
-        for j in range(cpt) if only is None else (only,):
-            c = t * cpt + j
-            p = piece(iw, t, j * prow)
+        for j in range(ppt) if only is None else (only,):
+            c = t * ppt + j
+            p = piece(iw, t, j * srow)
             for side, i in sides:
                 @pl.when(has[side])
                 def _():
                     rcopy(p, p, ag_s.at[i, 0, c], ag_r.at[i, 0, c], dev[side]).start()
 
     def relay(t, d):
-        for j in range(cpt):
-            c = t * cpt + j
+        for j in range(ppt):
+            c = t * ppt + j
             for side, i in sides:
                 src = iw - d if i == 0 else iw + d
                 here = src >= 0 if i == 0 else src < n_w
-                p = piece(src, t, j * prow)
+                p = piece(src, t, j * srow)
 
                 @pl.when(here)
                 def _():
@@ -457,13 +461,13 @@
         if pair:
             w_hand(d, mine).wait_send()
     for t in range(t_dev):
-        for j in range(cpt):
-            c = t * cpt + j
+        for j in range(ppt):
+            c = t * ppt + j
             for side, i in sides:
                 for d in range(n_w - 1):
                     src = iw - d if i == 0 else iw + d
                     here = src >= 0 if i == 0 else src < n_w
-                    p = piece(src, t, j * prow)
+                    p = piece(src, t, j * srow)
 
                     @pl.when(here & has[side])
                     def _():
@@ -488,7 +492,7 @@
     cw = conv_weight.reshape(3, 3, 3 * ch, ch)
     w2 = qkv_weight.transpose(1, 2, 0, 3).reshape(qkv_count, pd, hd)
     frames = n_t * t_dev
-    chunks = t_dev * (h_dev // CH)
+    chunks = t_dev * (h_dev // PH)
     vm = pl.BlockSpec(memory_space=pltpu.VMEM)
     hbm = pl.BlockSpec(memory_space=pltpu.HBM)
     dma = pltpu.SemaphoreType.DMA

time: 70.1 us -> 70.7 us (level)
  no operation moved by 1% of the time
where the time goes in v7:
time: 70.7 us; the launch traced here: 70.6 us
  Pallas kernels  69.9 us (99%)
    pallas_call x1, Pallas kernels, local(): pl.pallas_call(functools.partial(kernel, n_t, n_h, n_w), out_shape=(jax.S...  67.4 us
    pallas_call x1, Pallas kernels, local(): pl.pallas_call(results, out_shape=(jax.ShapeDtypeStruct(block_out.shape,...  2.55 us

profile of v7, /device:TPU:0, one launch (start us, length us, event | category | flops | bytes accessed | tf_op | source)
XLA Modules:
  0.0 70.6 jit_solution(5677771158309509853)
XLA Ops:
  0.6 67.4 %shard_map.59 = (bf16[2,16,32,256]{3,2,1,0:T(8,128)(2,1)}, bf16[8,8,64,128]{3,2,1,0:T(8,128)(2,1)}) custom-call(bf16[2,16,32,256]{3,2,1,0:T(8,128)(2,1)} %lat_hbm.1, f32[1,256]{1,0:T(1,128)} %bitcast.10, bf16[3,3,768,256]{3,2,1,0:T(8,128)(2,1)} %bitcast.8, bf16[3,1024,128]{2,1,0:T(8,128)(2,1)} %bitcast.9), custom_call_target="tpu_custom_call" | custom-call | tf_op jit(solution)/shard_map/pallas_call | solution.py:499
  68.0 2.5 %shard_map.60 = (bf16[2,16,32,256]{3,2,1,0:T(8,128)(2,1)}, bf16[8,8,64,128]{3,2,1,0:T(8,128)(2,1)}) custom-call(bf16[2,16,32,256]{3,2,1,0:T(8,128)(2,1)} %get-tuple-element.6.block, bf16[8,8,64,128]{3,2,1,0:T(8,128)(2,1)} %get-tuple-element.7.att), custom_call_target="tpu_custom_call" | custom-call | tf_op jit(solution)/shard_map/pallas_call | solution.py:538
